TPU v7x, 128 devices: a whole 4x4x4 slice. The times are simulated.
128 devices in a mesh: node: 16 (over x_lo, z, core), group: 8 (over x_hi, y).
Axes of the slice: x: 4 (x_hi: 2, x_lo: 2; x = x_hi * 2 + x_lo), y: 4, z: 4, core: 2. Of those that a mesh axis runs over, the one named last changes fastest.
Arguments:
- queries: bfloat16 [65536, 1024], P(('group', 'node')), may hold values from -10 to 10, as said below
- key_rows: bfloat16 [65536, 1024], P(('group', 'node')), may hold values from -10 to 10, as said below
- value_rows: bfloat16 [65536, 1024], P(('group', 'node')), may hold values from -10 to 10, as said below
- grad_output: bfloat16 [65536, 2048], P(('group', 'node')), may hold values from -6 to 6
- out_weight: bfloat16 [1024, 2048], replicated, may hold values from -0.1875 to 0.1875
Outputs:
- grad_queries: bfloat16 [65536, 1024], P(('group', 'node'))
- grad_keys: bfloat16 [65536, 1024], P(('group', 'node'))
- grad_values: bfloat16 [65536, 1024], P(('group', 'node'))
- grad_weight: float32 [1024, 2048], replicated
Inputs may be any that keep to these rules, and one draw needn't show every extreme that they name: `queries`: entries of order one. `key_rows`: entries of order one. `value_rows`: entries of order one.
All inputs are finite; a program needn't handle non-finite values.
Results may differ from a plain program's by a relative error of at most 0.018.
Values may be sent and summed in bfloat16 or wider, within the bound.
A program may use at most 128 MiB of HBM per device.

v0:
```python
import math

import jax
import jax.numpy as jnp
from jax import lax
from jax.sharding import PartitionSpec as P

HEADS = 8
HEAD_DIM = 128
LEAF = 128
S1 = 16
S2 = 256


NEG = -1e30


def coarsen(array, factor):
    width = array.shape[1]
    summed = jnp.mean(
        array.astype(jnp.float32).reshape(array.shape[0] // factor, factor, width), axis=1
    )
    return summed.astype(jnp.bfloat16)


def attend(
    query_blk,
    key_blk,
    value_blk,
    grad_blk,
    weight,
    near_keys,
    near_values,
    near_keep,
    far_keys,
    far_values,
    far_keep,
):
    row_count = query_blk.shape[0]
    head_count = HEADS
    head_width = HEAD_DIM
    pair_len = 2 * LEAF
    pair_count = row_count // pair_len
    inv_root = 1.0 / math.sqrt(head_width)
    wide = jnp.float32

    def to_pairs(array):
        return array.reshape(pair_count, pair_len, head_count, head_width)

    def to_heads(array):
        return array.reshape(array.shape[0], head_count, head_width)

    query_pair = to_pairs(query_blk)
    key_pair = to_pairs(key_blk)
    value_pair = to_pairs(value_blk)
    query_head = to_heads(query_blk)
    near_key_head = to_heads(near_keys)
    near_value_head = to_heads(near_values)
    far_key_head = to_heads(far_keys)
    far_value_head = to_heads(far_values)
    fine_score = (
        jnp.einsum("pqhd,pkhd->hpqk", query_pair, key_pair, preferred_element_type=wide).reshape(
            head_count, row_count, pair_len
        )
        * inv_root
    )
    near_score = jnp.where(
        near_keep[None],
        jnp.einsum("rhd,jhd->hrj", query_head, near_key_head, preferred_element_type=wide)
        * inv_root,
        NEG,
    )
    far_score = jnp.where(
        far_keep[None],
        jnp.einsum("rhd,jhd->hrj", query_head, far_key_head, preferred_element_type=wide)
        * inv_root,
        NEG,
    )
    row_max = jnp.maximum(jnp.maximum(fine_score.max(-1), near_score.max(-1)), far_score.max(-1))
    fine_exp = jnp.exp(fine_score - row_max[..., None])
    near_exp = jnp.exp(near_score - row_max[..., None])
    far_exp = jnp.exp(far_score - row_max[..., None])
    row_sum = fine_exp.sum(-1) + near_exp.sum(-1) + far_exp.sum(-1)
    fine_prob = fine_exp / row_sum[..., None]
    near_prob = near_exp / row_sum[..., None]
    far_prob = far_exp / row_sum[..., None]
    fine_low = fine_prob.astype(jnp.bfloat16).reshape(head_count, pair_count, pair_len, pair_len)
    near_low = near_prob.astype(jnp.bfloat16)
    far_low = far_prob.astype(jnp.bfloat16)
    fine_out = jnp.einsum(
        "hpqk,pkhd->pqhd", fine_low, value_pair, preferred_element_type=wide
    ).reshape(row_count, head_count, head_width)
    near_out = jnp.einsum("hrj,jhd->rhd", near_low, near_value_head, preferred_element_type=wide)
    far_out = jnp.einsum("hrj,jhd->rhd", far_low, far_value_head, preferred_element_type=wide)
    attended = (
        (fine_out + near_out + far_out)
        .reshape(row_count, head_count * head_width)
        .astype(jnp.bfloat16)
    )
    grad_attended = lax.dot_general(
        grad_blk, weight, (((1,), (1,)), ((), ())), preferred_element_type=wide
    ).astype(jnp.bfloat16)
    weight_part = lax.dot_general(
        attended, grad_blk, (((0,), (0,)), ((), ())), preferred_element_type=wide
    )
    row_delta = jnp.sum(
        to_heads(attended).astype(wide) * to_heads(grad_attended).astype(wide), axis=-1
    ).T
    grad_pair = to_pairs(grad_attended)
    grad_head = to_heads(grad_attended)
    fine_dprob = jnp.einsum(
        "pqhd,pkhd->hpqk", grad_pair, value_pair, preferred_element_type=wide
    ).reshape(head_count, row_count, pair_len)
    near_dprob = jnp.einsum("rhd,jhd->hrj", grad_head, near_value_head, preferred_element_type=wide)
    far_dprob = jnp.einsum("rhd,jhd->hrj", grad_head, far_value_head, preferred_element_type=wide)
    fine_dscore = (fine_prob * (fine_dprob - row_delta[..., None])).astype(jnp.bfloat16)
    near_dscore = (near_prob * (near_dprob - row_delta[..., None])).astype(jnp.bfloat16)
    far_dscore = (far_prob * (far_dprob - row_delta[..., None])).astype(jnp.bfloat16)
    fine_dfour = fine_dscore.reshape(head_count, pair_count, pair_len, pair_len)
    grad_query = jnp.einsum(
        "hpqk,pkhd->pqhd", fine_dfour, key_pair, preferred_element_type=wide
    ).reshape(row_count, head_count, head_width)
    grad_query = grad_query + jnp.einsum(
        "hrj,jhd->rhd", near_dscore, near_key_head, preferred_element_type=wide
    )
    grad_query = grad_query + jnp.einsum(
        "hrj,jhd->rhd", far_dscore, far_key_head, preferred_element_type=wide
    )
    grad_query = (grad_query * inv_root).reshape(row_count, -1).astype(jnp.bfloat16)
    fine_dkey = (
        jnp.einsum("hpqk,pqhd->pkhd", fine_dfour, query_pair, preferred_element_type=wide)
        * inv_root
    ).reshape(row_count, -1)
    fine_dvalue = jnp.einsum(
        "hpqk,pqhd->pkhd", fine_low, grad_pair, preferred_element_type=wide
    ).reshape(row_count, -1)
    near_dkey = (
        jnp.einsum("hrj,rhd->jhd", near_dscore, query_head, preferred_element_type=wide) * inv_root
    ).reshape(near_keys.shape[0], -1)
    near_dvalue = jnp.einsum(
        "hrj,rhd->jhd", near_low, grad_head, preferred_element_type=wide
    ).reshape(near_keys.shape[0], -1)
    far_dkey = (
        jnp.einsum("hrj,rhd->jhd", far_dscore, query_head, preferred_element_type=wide) * inv_root
    ).reshape(far_keys.shape[0], -1)
    far_dvalue = jnp.einsum(
        "hrj,rhd->jhd", far_low, grad_head, preferred_element_type=wide
    ).reshape(far_keys.shape[0], -1)
    return (
        grad_query,
        fine_dkey,
        fine_dvalue,
        near_dkey,
        near_dvalue,
        far_dkey,
        far_dvalue,
        weight_part,
    )


def body(queries, key_rows, value_rows, grad_output, out_weight):
    row_count = queries.shape[0]
    node_count = lax.axis_size("node")
    group_count = lax.axis_size("group")
    ratio = S2 // S1
    own_near_keys = coarsen(key_rows, S1)
    own_near_values = coarsen(value_rows, S1)
    near_keys, near_values = (
        lax.all_gather(own_near_keys, "node", axis=0, tiled=True),
        lax.all_gather(own_near_values, "node", axis=0, tiled=True),
    )
    position = lax.axis_index("node") * row_count + jnp.arange(row_count, dtype=jnp.int32)
    near_index = jnp.arange(near_keys.shape[0], dtype=jnp.int32)
    near_keep = near_index[None, :] * S1 // (2 * LEAF) != position[:, None] // (2 * LEAF)
    my_group = lax.axis_index("group")
    own_far_rows = row_count // S2
    own_far_keys = coarsen(own_near_keys, ratio)
    own_far_values = coarsen(own_near_values, ratio)
    far_keys, far_values = (
        lax.all_gather(own_far_keys, ("node", "group"), axis=0, tiled=True),
        lax.all_gather(own_far_values, ("node", "group"), axis=0, tiled=True),
    )
    source_piece = jnp.arange(far_keys.shape[0], dtype=jnp.int32) // own_far_keys.shape[0]
    far_keep = (source_piece % group_count != my_group)[None, :]
    loop_outputs = attend(
        queries,
        key_rows,
        value_rows,
        grad_output,
        out_weight,
        near_keys,
        near_values,
        near_keep,
        far_keys,
        far_values,
        far_keep,
    )
    (
        grad_queries,
        fine_dkey,
        fine_dvalue,
        near_dkey,
        near_dvalue,
        far_dkey,
        far_dvalue,
        weight_part,
    ) = loop_outputs
    width = far_dkey.shape[1]
    own_key_grad, own_value_grad = (
        lax.psum_scatter(
            near_dkey.astype(jnp.bfloat16), "node", scatter_dimension=0, tiled=True
        ).astype(jnp.float32),
        lax.psum_scatter(
            near_dvalue.astype(jnp.bfloat16), "node", scatter_dimension=0, tiled=True
        ).astype(jnp.float32),
    )
    far_kfour = far_dkey.reshape(node_count, group_count, own_far_rows, width)
    far_vfour = far_dvalue.reshape(node_count, group_count, own_far_rows, width)
    group_kpart, group_vpart = (
        lax.psum_scatter(
            far_kfour.astype(jnp.bfloat16), "group", scatter_dimension=1, tiled=True
        ).astype(jnp.float32),
        lax.psum_scatter(
            far_vfour.astype(jnp.bfloat16), "group", scatter_dimension=1, tiled=True
        ).astype(jnp.float32),
    )
    node_kpart, node_vpart = (
        lax.psum_scatter(
            group_kpart.astype(jnp.bfloat16), "node", scatter_dimension=0, tiled=True
        ).astype(jnp.float32),
        lax.psum_scatter(
            group_vpart.astype(jnp.bfloat16), "node", scatter_dimension=0, tiled=True
        ).astype(jnp.float32),
    )
    own_far_kgrad = node_kpart.reshape(own_far_rows, width)
    own_far_vgrad = node_vpart.reshape(own_far_rows, width)
    key_total = own_key_grad + jnp.repeat(own_far_kgrad / ratio, ratio, axis=0)
    value_total = own_value_grad + jnp.repeat(own_far_vgrad / ratio, ratio, axis=0)
    weight_total = lax.psum(weight_part, ("node", "group"))
    grad_weight = weight_total * (1.0 / math.sqrt(row_count * node_count * group_count))
    grad_keys = (fine_dkey + jnp.repeat(key_total / S1, S1, axis=0)).astype(jnp.bfloat16)
    grad_values = (fine_dvalue + jnp.repeat(value_total / S1, S1, axis=0)).astype(jnp.bfloat16)
    return (grad_queries, grad_keys, grad_values, grad_weight)


def solution(mesh):
    placed = (
        P(("group", "node"), None),
        P(("group", "node"), None),
        P(("group", "node"), None),
        P(("group", "node"), None),
        P(),
    )
    return jax.shard_map(
        body,
        mesh=mesh,
        in_specs=placed,
        out_specs=(
            P(("group", "node"), None),
            P(("group", "node"), None),
            P(("group", "node"), None),
            P(),
        ),
        check_vma=False,
    )
```

profile of v0, /device:TPU:0, one launch (start us, length us, event | category | flops | bytes accessed | tf_op | source)
XLA Modules:
  0.0 1272.0 jit_solution(13629634542947852074)
XLA Ops:
  7.2 1.8 convert_reduce_fusion.1
  9.7 1.6 convert_reduce_fusion
  12.2 320.8 %all-gather.1 = bf16[128,2,1024]{2,1,0:T(2,128)(2,1)S(1)} all-gather(bf16[1,2,1024]{2,1,0:T(2,128)(2,1)S(1)} %fusion.69), channel_id=1, replica_groups=mesh['node'=16,'group'=8] {'node','group'}, dimensions={0}, use_global_device_ids=true | all-gather | bytes 528384 | tf_op jit(solution)/shard_map/all_gather | solution.py:181
  333.0 1.2 reshape.291
  334.2 312.7 %all-gather = bf16[128,2,1024]{2,1,0:T(2,128)(2,1)S(1)} all-gather(bf16[1,2,1024]{2,1,0:T(2,128)(2,1)S(1)} %fusion.68), channel_id=1, replica_groups=mesh['node'=16,'group'=8] {'node','group'}, dimensions={0}, use_global_device_ids=true | all-gather | bytes 528384 | tf_op jit(solution)/shard_map/all_gather | solution.py:180
  647.2 1.1 copy.129
  648.4 5.6 convolution_convert_fusion
  654.0 2.3 copy.175
  656.5 2.9 copy.181
  659.7 2.7 multiply_reduce_fusion
  662.5 3.0 bitcast_reduce_fusion
  665.8 2.7 copy.101
  668.5 6.7 fusion.2
  675.2 3.1 fusion.7
  678.3 5.1 fusion.1
  683.5 3.1 fusion.5
  686.9 3.3 fusion.41
  690.3 2.2 copy.149
  692.4 1.9 convert_element_type.167
  694.4 2.2 copy.150
  696.5 3.1 fusion.59
  699.7 0.8 fusion.25
  700.4 2.6 copy.110
  703.0 3.0 copy.113
  706.1 2.5 copy.111
  708.6 5.3 fusion.15
  714.6 2.5 multiply_reduce_fusion.1
  717.1 1.4 multiply_convert_fusion.1
  719.7 1.2 copy.138
  720.9 1.9 convert_element_type.158
  722.9 2.2 copy.139
  725.1 46.9 %reduce-scatter.11.cloned.1.call-done = bf16[16,1,2,1024]{3,0,2,1:T(8,128)(2,1)} async-done(((bf16[16,8,2,1024]{3,0,2,1:T(8,128)(2,1)}), bf16[16,1,2,1024]{3,0,2,1:T(8,128)(2,1)}) %reduce-scatter.11.cloned.1.call-update) | async-done | bytes 65552 | tf_op jit(solution)/shard_map/reduce_scatter | solution.py:223
  772.0 1.5 copy.151
  773.5 71.6 %reduce-scatter.9.cloned.1.call-done = bf16[16,1,2,1024]{3,0,2,1:T(8,128)(2,1)} async-done(((bf16[16,8,2,1024]{3,0,2,1:T(8,128)(2,1)}), bf16[16,1,2,1024]{3,0,2,1:T(8,128)(2,1)}) %reduce-scatter.9.cloned.1.call-update) | async-done | bytes 65552 | tf_op jit(solution)/shard_map/reduce_scatter | solution.py:220
  845.1 1.5 copy.140
  846.7 7.2 fusion.36
  854.0 2.3 copy.173
  856.4 7.2 multiply_convert_fusion
  863.6 2.5 multiply_convert_fusion.3
  866.1 2.2 copy.171
  868.6 7.0 fusion.83
  875.6 2.5 copy.180
  878.7 4.1 fusion.28
  882.8 2.9 copy.143
  885.7 4.2 multiply_convert_fusion.2
  889.9 0.8 fusion.31
  890.7 2.5 copy.120
  893.2 3.0 copy.125
  896.2 2.3 fusion.82
  898.6 4.1 fusion.11
  902.6 2.3 copy.152
  904.9 2.6 multiply_bitcast_fusion
  907.5 2.6 copy.133
  910.0 52.3 %all-reduce.8.cloned.1.call-done = (bf16[16,1,2,1024]{3,2,1,0:T(2,128)(2,1)}, bf16[16,1,2,1024]{3,2,1,0:T(2,128)(2,1)}) async-done(((bf16[16,1,2,1024]{3,2,1,0:T(2,128)(2,1)}, bf16[16,1,2,1024]{3,2,1,0:T(2,128)(2,1)}), (bf16[16,1,2,1024]{3,2,1,0:T(2,128)(2,1)}, bf16[16,1,2,1024]{3,2,1,0:T(2,128)(2,1)})) %all-reduce.8.cloned.1.call-update) | async-done | bytes 131088
  962.4 1.3 multiply_bitcast_fusion.2
  963.7 1.3 multiply_bitcast_fusion.1
  965.0 62.5 %reduce-scatter.15.cloned.1.call-done = bf16[32,1024]{1,0:T(8,128)(2,1)} async-done(((bf16[512,1024]{1,0:T(8,128)(2,1)}), bf16[32,1024]{1,0:T(8,128)(2,1)}) %reduce-scatter.15.cloned.1.call-update) | async-done | bytes 65552 | tf_op jit(solution)/shard_map/reduce_scatter | solution.py:213
  1027.4 0.9 fusion.66
  1028.3 2.9 fusion.8
  1031.2 58.7 %reduce-scatter.13.cloned.1.call-done = bf16[32,1024]{1,0:T(8,128)(2,1)} async-done(((bf16[512,1024]{1,0:T(8,128)(2,1)}), bf16[32,1024]{1,0:T(8,128)(2,1)}) %reduce-scatter.13.cloned.1.call-update) | async-done | bytes 65552 | tf_op jit(solution)/shard_map/reduce_scatter | solution.py:210
  1089.9 0.9 fusion.67
  1090.8 2.9 fusion.9
  1093.7 162.8 %all-reduce.6.cloned.1.call-done = f32[1024,2048]{1,0:T(8,128)} async-done(((f32[1024,2048]{1,0:T(8,128)}), f32[1024,2048]{1,0:T(8,128)}) %all-reduce.6.cloned.1.call-update) | async-done | bytes 8388624 | tf_op jit(solution)/shard_map/psum | solution.py:239
  1256.5 8.4 broadcast_multiply_fusion
  (87 shorter events, 6.2 us)
Async XLA Ops:
  7.2 641.2 %copy-start = (bf16[512,2048]{1,0:T(8,128)(2,1)S(1)}, bf16[512,2048]{1,0:T(8,128)(2,1)}, u32[]{:S(2)}) copy-start(bf16[512,2048]{1,0:T(8,128)(2,1)} %param.8) | copy-start | bytes 6291460
  7.2 658.6 %all-gather.5.cloned.1.call-start = ((), (), s32[]{:S(2)}) async-start(), calls=%async_computation.4 | async-start | bytes 1114112 | tf_op jit(solution)/shard_map/all_gather | solution.py:169
  9.7 696.4 %all-gather.7.cloned.1.call-start = ((), (), s32[]{:S(2)}) async-start(), calls=%async_computation.5 | async-start | bytes 1114112 | tf_op jit(solution)/shard_map/all_gather | solution.py:170
  12.0 759.9 %reduce-scatter.11.cloned.1.call-start = ((), (), s32[]{:S(2)}) async-start(), calls=%async_computation.7 | async-start | bytes 589824 | tf_op jit(solution)/shard_map/reduce_scatter | solution.py:223
  12.1 663.1 %copy-start.20 = (pred[256]{0:T(512)(128)(4,1)}, pred[256]{0:T(512)(128)(4,1)S(1)}, u32[]{:S(2)}) copy-start(pred[256]{0:T(512)(128)(4,1)S(1)} %fusion.77) | copy-start | bytes 772
  648.4 7.9 copy-start.5
  656.2 3.2 copy-start.13
  656.5 5.9 copy-start.14
  659.4 3.0 copy-start.6
  659.4 3.0 copy-start.10
  683.5 3.5 copy-start.2
  696.5 3.1 copy-start.11
  699.6 3.4 copy-start.1
  706.0 139.1 %reduce-scatter.9.cloned.1.call-start = ((), (), s32[]{:S(2)}) async-start(), calls=%async_computation.6 | async-start | bytes 589824 | tf_op jit(solution)/shard_map/reduce_scatter | solution.py:220
  708.6 5.3 copy-start.3
  708.6 5.7 copy-start.17
  708.6 5.9 copy-start.18
  708.6 6.0 copy-start.19
  708.6 6.0 copy-start.21
  717.0 1.4 copy-start.7
  718.4 1.3 copy-start.15
  725.0 237.3 %all-reduce.8.cloned.1.call-start = ((), (), s32[]{:S(2)}) async-start(), calls=%async_computation.11 | async-start | bytes 262144
  846.7 180.8 %reduce-scatter.15.cloned.1.call-start = ((), (), s32[]{:S(2)}) async-start(), calls=%async_computation.10 | async-start | bytes 1114112 | tf_op jit(solution)/shard_map/reduce_scatter | solution.py:213
  856.3 233.6 %reduce-scatter.13.cloned.1.call-start = ((), (), s32[]{:S(2)}) async-start(), calls=%async_computation.9 | async-start | bytes 1114112 | tf_op jit(solution)/shard_map/reduce_scatter | solution.py:210
  856.3 7.2 copy-start.8
  863.6 2.5 copy-start.12
  868.3 388.2 %all-reduce.6.cloned.1.call-start = ((), (), s32[]{:S(2)}) async-start(), calls=%async_computation.8 | async-start | bytes 16777216 | tf_op jit(solution)/shard_map/psum | solution.py:239
  875.6 2.5 copy-start.22
  889.9 3.3 copy-start.16
  893.2 5.3 copy-start.4
  896.2 2.4 copy-start.9
Sparse Core Ops, SparseCore 0:
  10.3 35.0 all-gather.4
  47.1 32.5 all-gather.6
  706.1 65.7 reduce-scatter.10
  775.8 69.3 reduce-scatter.8
  847.5 114.8 all-reduce.7
  964.7 62.6 reduce-scatter.14
  1029.8 60.0 reduce-scatter.12
  1096.3 160.1 all-reduce.5
where the time goes:
time: 1280 us; the launch traced here: 1270 us
  blocking collectives  634 us (50%)
  waiting for transfers between devices  455 us (36%)
  matrix products  73.8 us (6%)
  local copies, waits for them, and re-layouts  56.4 us (4%)
  other arithmetic  38 us (3%)
  between operations  14.8 us (1%)
    all_gather x1, blocking collectives, body(): lax.all_gather(own_far_values, ('node', 'group'), axis=0, tiled=True)  321 us
    all_gather x1, blocking collectives, body(): lax.all_gather(own_far_keys, ('node', 'group'), axis=0, tiled=True)  313 us
    psum x1, waiting for transfers between devices, body(): weight_total = lax.psum(weight_part, ('node', 'group'))  163 us
    reduce_scatter x1, waiting for transfers between devices, body(): lax.psum_scatter(far_kfour.astype(jnp.bfloat16), 'group', scatter_dimensi...  71.6 us
    reduce_scatter x1, waiting for transfers between devices, body(): lax.psum_scatter(near_dvalue.astype(jnp.bfloat16), 'node', scatter_dimens...  62.5 us
    reduce_scatter x1, waiting for transfers between devices, body(): lax.psum_scatter(near_dkey.astype(jnp.bfloat16), 'node', scatter_dimensio...  58.7 us
    unnamed x9, waiting for transfers between devices  52.4 us
    reduce_scatter x1, waiting for transfers between devices, body(): lax.psum_scatter(far_vfour.astype(jnp.bfloat16), 'group', scatter_dimensi...  46.9 us
  transfers between devices with their start and end apart: 8, of which 6 were waited for; matrix products, arithmetic and copies ran while one was open for 12% of the time, Pallas kernels for 0%

commit v1 on v0

v1 whole, which is shorter than its diff:
```python
import math

import jax
import jax.numpy as jnp
from jax import lax
from jax.experimental import pallas as pl
from jax.experimental.pallas import tpu as pltpu
from jax.sharding import PartitionSpec as P

HEADS = 8
WIDTH = 128
S1 = 16
ROWS = 512
PAIR = 256
CHIPS = 8
SLOT = 48
KEYS = 768
COLS = 2048
CLASSES = ((0, 3), (3, 3), (6, 2))
BF = jnp.bfloat16
F32 = jnp.float32
SCALE = 1.0 / math.sqrt(WIDTH)
EXP2_SCALE = math.log2(math.e) / math.sqrt(WIDTH)


def dot(a, b, ca, cb):
    return lax.dot_general(a, b, (((ca,), (cb,)), ((), ())), preferred_element_type=F32)


def flip4(a, d):
    if d == 0:
        return a
    if d == 1:
        return a + 1 - 2 * (a % 2)
    if d == 2:
        return (a + 2) % 4
    return 3 - a


def flip2(a, d):
    return 1 - a if d else a


class Place:
    def __init__(self):
        node = lax.axis_index("node")
        group = lax.axis_index("group")
        self.node, self.group = node, group
        self.core = node % 2
        self.z = (node // 2) % 4
        self.x_lo = node // 8
        self.x_hi = group // 4
        self.y = group % 4

    def coord(self, axis):
        return (self.x_hi * 2 + self.x_lo, self.y, self.z)[axis]

    def at(self, x_lo, x_hi, y, z, core):
        return {"node": (x_lo * 4 + z) * 2 + core, "group": x_hi * 4 + y}

    def sibling(self):
        return self.at(self.x_lo, self.x_hi, self.y, self.z, 1 - self.core)

    def chip(self, c):
        return self.at(
            flip2(self.x_lo, c // 4), self.x_hi, self.y, flip4(self.z, c % 4), self.core
        )

    def peer_group(self, j):
        return self.at(
            self.x_lo, flip2(self.x_hi, j // 4), flip4(self.y, j % 4), self.z, self.core
        )

    def along(self, axis, d):
        if axis == 0:
            return self.at(
                flip2(self.x_lo, d % 2), flip2(self.x_hi, d // 2), self.y, self.z, self.core
            )
        if axis == 1:
            return self.at(self.x_lo, self.x_hi, flip4(self.y, d), self.z, self.core)
        return self.at(self.x_lo, self.x_hi, self.y, flip4(self.z, d), self.core)


def send(src, dst, send_sem, recv_sem, device):
    copy = pltpu.make_async_remote_copy(
        src_ref=src,
        dst_ref=dst,
        send_sem=send_sem,
        recv_sem=recv_sem,
        device_id=device,
        device_id_type=pl.DeviceIdType.MESH,
    )
    copy.start()
    return copy


def kernel(
    q_ref, k_ref, v_ref, go_ref, w_ref,
    gq_ref, gk_ref, gv_ref, wout,
    nf, fx_send, fx, far_blk, gt, att, probs, gst, gs, delta,
    gnf, cr, snd, rr, fine_k, fine_v, tot, fb_send, fb,
    wpart, wr0, ra, rb, rc, sa, sb,
    near_ss, near_rs, far_ss, far_rs, fx_ss, fx_rs,
    g_ss, g_rs, w_ss, w_rs, core_ss, core_rs, fb_ss, fb_rs,
):
    me = Place()
    core = me.core

    barrier = pltpu.get_barrier_semaphore()
    partners = [me.sibling()]
    partners += [me.chip(c) for c in range(1, CHIPS)]
    partners += [me.peer_group(j) for j in range(1, 8)]
    partners += [me.along(0, 3)]
    for partner in partners:
        pl.semaphore_signal(barrier, inc=1, device_id=partner, device_id_type=pl.DeviceIdType.MESH)

    rows = lax.broadcasted_iota(jnp.int32, (32, ROWS), 0)
    toks = lax.broadcasted_iota(jnp.int32, (32, ROWS), 1)
    mean16 = jnp.where(toks // S1 == rows, 1.0 / S1, 0.0).astype(BF)
    near_k = dot(mean16, k_ref[...], 1, 0).astype(BF)
    near_v = dot(mean16, v_ref[...], 1, 0).astype(BF)
    nf[0, 0:32, :] = near_k
    nf[1, 0:32, :] = near_v
    r8 = lax.broadcasted_iota(jnp.int32, (8, 32), 0)
    c8 = lax.broadcasted_iota(jnp.int32, (8, 32), 1) // 16
    pick_k = jnp.where(c8 == r8, 1.0 / S1, 0.0).astype(BF)
    pick_v = jnp.where(c8 + 2 == r8, 1.0 / S1, 0.0).astype(BF)
    far_own = (dot(pick_k, near_k, 1, 0) + dot(pick_v, near_v, 1, 0)).astype(BF).astype(F32)
    fx_send[...] = far_own

    pl.semaphore_wait(barrier, len(partners))

    fx_copies = []
    for j in range(1, 8):
        fx_copies.append(
            send(fx_send, fx.at[j], fx_ss.at[j], fx_rs.at[j], me.peer_group(j))
        )
    near_copies = [None]
    for c in range(1, CHIPS):
        near_copies.append(
            send(
                nf.at[:, pl.ds(0, 32), :],
                nf.at[:, pl.ds(SLOT * c, 32), :],
                near_ss.at[c],
                near_rs.at[c],
                me.chip(c),
            )
        )
    near_fwd = [
        send(
            nf.at[:, pl.ds(0, 32), :],
            nf.at[:, pl.ds(SLOT * CHIPS, 32), :],
            near_ss.at[CHIPS],
            near_rs.at[CHIPS],
            me.sibling(),
        )
    ]

    def project(i, carry):
        r = pl.ds(pl.multiple_of(i * 256, 256), 256)
        gt[r, :] = dot(w_ref[r, :], go_ref[...], 1, 1).astype(BF)
        return carry

    lax.fori_loop(0, 4, project, 0)

    for j in range(1, 8):
        fx_copies[j - 1].wait()
    far_blk[0, 0:2, :] = far_own[0:2]
    far_blk[1, 0:2, :] = far_own[2:4]
    for j in range(1, 8):
        far_blk[0, 2 * j : 2 * j + 2, :] = fx[j, 0:2, :]
        far_blk[1, 2 * j : 2 * j + 2, :] = fx[j, 2:4, :]
    nf[:, 32:48, :] = far_blk[...].astype(BF)
    far_copies = [None]
    for c in range(1, CHIPS):
        far_copies.append(
            send(
                nf.at[:, pl.ds(32, 16), :],
                nf.at[:, pl.ds(SLOT * c + 32, 16), :],
                far_ss.at[c],
                far_rs.at[c],
                me.chip(c),
            )
        )
    far_fwd = [
        send(
            nf.at[:, pl.ds(32, 16), :],
            nf.at[:, pl.ds(SLOT * CHIPS + 32, 16), :],
            far_ss.at[CHIPS],
            far_rs.at[CHIPS],
            me.sibling(),
        )
    ]
    for c in range(1, CHIPS):
        near_copies[c].wait()
        near_fwd.append(
            send(
                nf.at[:, pl.ds(SLOT * c, 32), :],
                nf.at[:, pl.ds(SLOT * (CHIPS + c), 32), :],
                near_ss.at[CHIPS + c],
                near_rs.at[CHIPS + c],
                me.sibling(),
            )
        )
    for c in range(1, CHIPS):
        far_copies[c].wait()
        far_fwd.append(
            send(
                nf.at[:, pl.ds(SLOT * c + 32, 16), :],
                nf.at[:, pl.ds(SLOT * (CHIPS + c) + 32, 16), :],
                far_ss.at[CHIPS + c],
                far_rs.at[CHIPS + c],
                me.sibling(),
            )
        )
    for c in range(CHIPS):
        near_fwd[c].wait()
        far_fwd[c].wait()

    row = lax.broadcasted_iota(jnp.int32, (KEYS, ROWS), 0)
    col = lax.broadcasted_iota(jnp.int32, (KEYS, ROWS), 1)
    hidden = (row % SLOT >= 32) & (row % SLOT < 34)
    hidden = hidden | ((row < 32) & (row // S1 == col // PAIR))

    def forward(h, carry):
        c = pl.ds(pl.multiple_of(h * WIDTH, WIDTH), WIDTH)
        qh = q_ref[:, c]
        s = dot(nf[0, :, c], qh, 1, 1)
        sf = [
            dot(k_ref[p * PAIR : (p + 1) * PAIR, c], qh[p * PAIR : (p + 1) * PAIR], 1, 1)
            for p in range(2)
        ]
        sf = jnp.concatenate(sf, axis=1)
        top = jnp.maximum(jnp.max(s, axis=0, keepdims=True), jnp.max(sf, axis=0, keepdims=True))
        e = jnp.exp2((s - top) * EXP2_SCALE)
        e = jnp.where(hidden, 0.0, e)
        ef = jnp.exp2((sf - top) * EXP2_SCALE)
        total = jnp.sum(e, axis=0, keepdims=True) + jnp.sum(ef, axis=0, keepdims=True)
        e = e.astype(BF)
        ef = ef.astype(BF)
        probs[h, 0:KEYS, :] = e
        probs[h, KEYS : KEYS + PAIR, :] = ef
        out = dot(nf[1, :, c], e, 0, 0)
        of = [
            dot(v_ref[p * PAIR : (p + 1) * PAIR, c], ef[:, p * PAIR : (p + 1) * PAIR], 0, 0)
            for p in range(2)
        ]
        out = out + jnp.concatenate(of, axis=1)
        inv = 1.0 / total
        out = (out * inv).astype(BF)
        att[c, :] = out
        gth = gt[c, :].astype(F32)
        d = jnp.sum(out.astype(F32) * gth, axis=0, keepdims=True) * inv
        delta[h] = jnp.broadcast_to(d, (8, ROWS))
        scaled = gth * inv
        gst[c, :] = scaled.astype(BF)
        gs[:, c] = scaled.T.astype(BF)
        return carry

    lax.fori_loop(0, HEADS, forward, 0)

    def weigh(i, carry):
        c = pl.ds(pl.multiple_of(i * 512, 512), 512)
        part = dot(att[...], go_ref[:, c], 1, 0)
        wpart[:, :, c] = part.reshape(HEADS, WIDTH, 512).astype(BF)
        return carry

    lax.fori_loop(0, 4, weigh, 0)

    def backward(h, carry):
        c = pl.ds(pl.multiple_of(h * WIDTH, WIDTH), WIDTH)
        qh = q_ref[:, c]
        gth = gst[c, :]
        gh = gs[:, c]
        d = delta[h, 0:1, :]
        kk = nf[0, :, c]
        e = probs[h, 0:KEYS, :]
        ds = (e.astype(F32) * (dot(nf[1, :, c], gth, 1, 0) - d)).astype(BF)
        gnf[1, :, c] = dot(e, gh, 1, 0).astype(BF)
        gnf[0, :, c] = (dot(ds, qh, 1, 0) * SCALE).astype(BF)
        dq = dot(kk, ds, 0, 0)
        dqf = []
        for p in range(2):
            r = slice(p * PAIR, (p + 1) * PAIR)
            ef = probs[h, KEYS : KEYS + PAIR, r]
            dsf = (ef.astype(F32) * (dot(v_ref[r, c], gth[:, r], 1, 0) - d[:, r])).astype(BF)
            fine_v[r, c] = dot(ef, gh[r], 1, 0)
            fine_k[r, c] = dot(dsf, qh[r], 1, 0) * SCALE
            dqf.append(dot(k_ref[r, c], dsf, 0, 0))
        dq = (dq + jnp.concatenate(dqf, axis=1)) * SCALE
        gq_ref[:, c] = dq.T.astype(BF)
        return carry

    lax.fori_loop(0, HEADS, backward, 0)

    half = CHIPS * SLOT
    to_sib = send(
        gnf.at[:, pl.ds(half, half), :], cr, core_ss.at[0], core_rs.at[0], me.sibling()
    )
    mine = pl.multiple_of(core * 64, 64)
    other = pl.multiple_of((1 - core) * 64, 64)
    w_sib = send(
        wpart.at[:, pl.ds(other, 64), :], wr0, core_ss.at[1], core_rs.at[1], me.sibling()
    )
    w_sib.wait()

    def add_core(h, carry):
        r = pl.ds(mine, 64)
        wpart[h, r, :] = (wpart[h, r, :].astype(F32) + wr0[h].astype(F32)).astype(BF)
        return carry

    lax.fori_loop(0, HEADS, add_core, 0)

    order = [[(cls + step) % 3 for step in range(3)] for cls in range(3)]

    def xor_coord(axis, d):
        if axis == 0:
            return flip2(me.x_hi, d // 2) * 2 + flip2(me.x_lo, d % 2)
        return flip4(me.coord(axis), d)

    def rs_a(cls):
        h0, hn = CLASSES[cls]
        axis = order[cls][0]
        return [
            send(
                wpart.at[
                    pl.ds(h0, hn), pl.ds(pl.multiple_of(mine + xor_coord(axis, d) * 16, 16), 16), :
                ],
                ra.at[d - 1, pl.ds(h0, hn)],
                w_ss.at[0, cls, d - 1],
                w_rs.at[0, cls, d - 1],
                me.along(axis, d),
            )
            for d in range(1, 4)
        ]

    def rs_b(cls):
        h0, hn = CLASSES[cls]
        axis = order[cls][1]
        return [
            send(
                sa.at[
                    pl.ds(h0, hn), :, pl.ds(pl.multiple_of(xor_coord(axis, d) * 512, 512), 512)
                ],
                rb.at[d - 1, pl.ds(h0, hn)],
                w_ss.at[1, cls, d - 1],
                w_rs.at[1, cls, d - 1],
                me.along(axis, d),
            )
            for d in range(1, 4)
        ]

    def rs_c(cls):
        h0, hn = CLASSES[cls]
        axis = order[cls][2]
        return [
            send(
                sb.at[
                    pl.ds(h0, hn), :, pl.ds(pl.multiple_of(xor_coord(axis, d) * 128, 128), 128)
                ],
                rc.at[d - 1, pl.ds(h0, hn)],
                w_ss.at[2, cls, d - 1],
                w_rs.at[2, cls, d - 1],
                me.along(axis, d),
            )
            for d in range(1, 4)
        ]

    def spot(cls):
        a, b, c = [me.coord(axis) for axis in order[cls]]
        return (
            pl.multiple_of(mine + a * 16, 16),
            pl.multiple_of(b * 512, 512),
            pl.multiple_of(b * 512 + c * 128, 128),
        )

    def gather(cls, step):
        h0, hn = CLASSES[cls]
        hs = pl.ds(h0, hn)
        row0, col_b, col_c = spot(cls)
        if step == 2:
            piece = wout.at[hs, pl.ds(row0, 16), pl.ds(col_c, 128)]
        elif step == 1:
            piece = wout.at[hs, pl.ds(row0, 16), pl.ds(col_b, 512)]
        else:
            piece = wout.at[hs, pl.ds(row0, 16), :]
        axis = order[cls][step]
        return [
            send(
                piece, piece, w_ss.at[5 - step, cls, d - 1], w_rs.at[5 - step, cls, d - 1],
                me.along(axis, d),
            )
            for d in range(1, 4)
        ]

    copies = [rs_a(cls) for cls in range(3)]

    to_sib.wait()
    for i in range(2):
        snd[i] = (gnf[i, 0:half, :].astype(F32) + cr[i].astype(F32)).astype(BF)
    near_rs_copies = []
    for c in range(1, CHIPS):
        near_rs_copies.append(
            send(
                snd.at[:, pl.ds(SLOT * c, SLOT), :],
                rr.at[c],
                g_ss.at[c],
                g_rs.at[c],
                me.chip(c),
            )
        )

    next_copies = []
    for cls in range(3):
        h0, hn = CLASSES[cls]
        for copy in copies[cls]:
            copy.wait()
        row0, _, _ = spot(cls)
        for h in range(h0, h0 + hn):
            t = wpart[h, pl.ds(row0, 16), :].astype(F32)
            for d in range(3):
                t = t + ra[d, h].astype(F32)
            sa[h] = t.astype(BF)
        next_copies.append(rs_b(cls))
    copies, next_copies = next_copies, []
    for cls in range(3):
        h0, hn = CLASSES[cls]
        for copy in copies[cls]:
            copy.wait()
        _, col_b, _ = spot(cls)
        hs = slice(h0, h0 + hn)
        t = sa[hs, :, pl.ds(col_b, 512)].astype(F32)
        for d in range(3):
            t = t + rb[d, hs].astype(F32)
        sb[hs] = t.astype(BF)
        next_copies.append(rs_c(cls))
    copies, next_copies = next_copies, []
    for cls in range(3):
        h0, hn = CLASSES[cls]
        for copy in copies[cls]:
            copy.wait()
        row0, _, col_c = spot(cls)
        hs = slice(h0, h0 + hn)
        c0 = pl.multiple_of(me.coord(order[cls][2]) * 128, 128)
        t = sb[hs, :, pl.ds(c0, 128)].astype(F32)
        for d in range(3):
            t = t + rc[d, hs].astype(F32)
        wout[hs, pl.ds(row0, 16), pl.ds(col_c, 128)] = t.astype(BF)
        next_copies.append(gather(cls, 2))
    copies, next_copies = next_copies, []

    for c in range(1, CHIPS):
        near_rs_copies[c - 1].wait()
    for i in range(2):
        t = snd[i, 0:SLOT, :].astype(F32)
        for c in range(1, CHIPS):
            t = t + rr[c, i].astype(F32)
        tot[i] = t
    for j in range(1, 8):
        fb_send[j, 0:2, :] = tot[0, 32 + 2 * j : 34 + 2 * j, :]
        fb_send[j, 2:4, :] = tot[1, 32 + 2 * j : 34 + 2 * j, :]
        fb_send[j, 4:8, :] = jnp.zeros((4, HEADS * WIDTH), F32)
    far_back = [
        send(fb_send.at[j], fb.at[j], fb_ss.at[j], fb_rs.at[j], me.peer_group(j))
        for j in range(1, 8)
    ]

    for step in (1, 0):
        for cls in range(3):
            for copy in copies[cls]:
                copy.wait()
            next_copies.append(gather(cls, step))
        copies, next_copies = next_copies, []
    for cls in range(3):
        for copy in copies[cls]:
            copy.wait()
    piece = wout.at[:, pl.ds(mine, 64), :]
    last = send(piece, piece, core_ss.at[2], core_rs.at[2], me.sibling())

    for copy in far_back:
        copy.wait()
    far_sum = fb[1]
    for j in range(2, 8):
        far_sum = far_sum + fb[j]
    far_sum = far_sum * (1.0 / (S1 * S1))
    for i in range(2):
        for r in range(2):
            part = tot[i, 16 * r : 16 * r + 16, :] * (1.0 / S1)
            tot[i, 16 * r : 16 * r + 16, :] = part + far_sum[2 * i + r : 2 * i + r + 1, :]

    def finish(i, carry):
        r = pl.ds(pl.multiple_of(i * S1, S1), S1)
        gk_ref[r, :] = (fine_k[r, :] + tot[0, pl.ds(i, 1), :]).astype(BF)
        gv_ref[r, :] = (fine_v[r, :] + tot[1, pl.ds(i, 1), :]).astype(BF)
        return carry

    lax.fori_loop(0, ROWS // S1, finish, 0)
    last.wait()


def body(queries, key_rows, value_rows, grad_output, out_weight):
    width = HEADS * WIDTH
    vmem = pltpu.VMEM
    dma = pltpu.SemaphoreType.DMA
    scratch = [
        vmem((2, KEYS, width), BF),
        vmem((8, width), F32),
        vmem((8, 8, width), F32),
        vmem((2, 16, width), F32),
        vmem((width, ROWS), BF),
        vmem((width, ROWS), BF),
        vmem((HEADS, KEYS + PAIR, ROWS), BF),
        vmem((width, ROWS), BF),
        vmem((ROWS, width), BF),
        vmem((HEADS, 8, ROWS), F32),
        vmem((2, KEYS, width), BF),
        vmem((2, CHIPS * SLOT, width), BF),
        vmem((2, CHIPS * SLOT, width), BF),
        vmem((CHIPS, 2, SLOT, width), BF),
        vmem((ROWS, width), F32),
        vmem((ROWS, width), F32),
        vmem((2, SLOT, width), F32),
        vmem((8, 8, width), F32),
        vmem((8, 8, width), F32),
        vmem((HEADS, WIDTH, COLS), BF),
        vmem((HEADS, 64, COLS), BF),
        vmem((3, HEADS, 16, COLS), BF),
        vmem((3, HEADS, 16, 512), BF),
        vmem((3, HEADS, 16, 128), BF),
        vmem((HEADS, 16, COLS), BF),
        vmem((HEADS, 16, 512), BF),
        dma((16,)), dma((16,)), dma((16,)), dma((16,)), dma((8,)), dma((8,)),
        dma((8,)), dma((8,)), dma((6, 3, 3)), dma((6, 3, 3)), dma((3,)), dma((3,)),
        dma((8,)), dma((8,)),
    ]
    spec = pl.BlockSpec(memory_space=pltpu.VMEM)
    gq, gk, gv, weight = pl.pallas_call(
        kernel,
        out_shape=(
            jax.ShapeDtypeStruct((ROWS, width), BF),
            jax.ShapeDtypeStruct((ROWS, width), BF),
            jax.ShapeDtypeStruct((ROWS, width), BF),
            jax.ShapeDtypeStruct((HEADS, WIDTH, COLS), BF),
        ),
        in_specs=[spec] * 5,
        out_specs=(spec,) * 4,
        scratch_shapes=scratch,
        compiler_params=pltpu.CompilerParams(
            collective_id=0, has_side_effects=True, vmem_limit_bytes=64 * 1024 * 1024 - 65536
        ),
        name="fused",
    )(queries, key_rows, value_rows, grad_output, out_weight)
    tokens = ROWS * lax.axis_size("node") * lax.axis_size("group")
    weight = weight.reshape(width, COLS).astype(F32) * (1.0 / math.sqrt(tokens))
    return gq, gk, gv, weight


def solution(mesh):
    split = P(("group", "node"), None)
    return jax.shard_map(
        body,
        mesh=mesh,
        in_specs=(split, split, split, split, P()),
        out_specs=(split, split, split, P()),
        check_vma=False,
    )
```

time: 1280 us -> 140 us (0.11)
  blocking collectives: 634 us -> 0 us
  waiting for transfers between devices: 455 us -> 0 us
  Pallas kernels: 0 us -> 128 us
  matrix products: 73.8 us -> 0 us
  local copies, waits for them, and re-layouts: 56.4 us -> 2.92 us
  other arithmetic: 38 us -> 6.93 us
  between operations: 14.8 us -> 0.67 us
    all_gather x2 -> x0, blocking collectives: 634 us -> none  [the longest x1 321 us: body(): lax.all_gather(own_far_values, ('node', 'group'), axis=0, tiled=True)]
    reduce_scatter x4 -> x0, waiting for transfers between devices: 240 us -> none  [the longest x1 71.6 us: body(): lax.psum_scatter(far_kfour.astype(jnp.bfloat16), 'group', scatter_dimensi...]
    psum x1 -> x0, waiting for transfers between devices: 163 us -> none  [body(): weight_total = lax.psum(weight_part, ('node', 'group'))]
    pallas_call x0 -> x1, Pallas kernels: none -> 128 us  [body(): pl.pallas_call(kernel, out_shape=(jax.ShapeDtypeStruct((ROWS, width), BF)...]
    dot_general x20 -> x0, matrix products: 73.8 us -> none  [the longest x1 7.24 us: attend(): jnp.einsum('hrj,rhd->jhd', near_low, grad_head, preferred_element_type=wide)]
    unnamed x9 -> x0, waiting for transfers between devices: 52.4 us -> none
    reduce_sum x7 -> x0, other arithmetic: 16 us -> none  [the longest x3 11.3 us: attend(): row_sum = fine_exp.sum(-1) + near_exp.sum(-1) + far_exp.sum(-1)]
  transfers between devices with their start and end apart: 8 -> 0, of which waited for: 6 -> 0; matrix products, arithmetic and copies ran while one was open for 12% -> 0% of each run, Pallas kernels for 0% -> 0%
where the time goes in v1:
time: 140 us; the launch traced here: 138 us
  Pallas kernels  128 us (91%)
  other arithmetic  6.93 us (5%)
  local copies, waits for them, and re-layouts  2.92 us (2%)
    pallas_call x1, Pallas kernels, body(): pl.pallas_call(kernel, out_shape=(jax.ShapeDtypeStruct((ROWS, width), BF)...  128 us
    mul x1, other arithmetic, body(): weight = weight.reshape(width, COLS).astype(F32) * (1.0 / math.sqrt(tokens))  6.93 us
    unnamed x9, local copies, waits for them, and re-layouts  2.92 us

profile of v1, /device:TPU:0, one launch (start us, length us, event | category | flops | bytes accessed | tf_op | source)
XLA Modules:
  0.0 138.4 jit_solution(11552784182600099523)
XLA Ops:
  0.6 127.9 %fused.1 = (bf16[512,1024]{1,0:T(8,128)(2,1)}, bf16[512,1024]{1,0:T(8,128)(2,1)}, bf16[512,1024]{1,0:T(8,128)(2,1)}, bf16[8,128,2048]{2,1,0:T(8,128)(2,1)}) custom-call(bf16[512,1024]{1,0:T(8,128)(2,1)} %q_ref.1, bf16[512,1024]{1,0:T(8,128)(2,1)} %k_ref.1, bf16[512,1024]{1,0:T(8,128)(2,1)} %v_ref.1, bf16[512,2048]{1,0:T(8,128)(2,1)} %go_ref.1, ...), custom_call_target="tpu_custom_call" | custom-call | tf_op jit(solution)/shard_map/fused/pallas_call | solution.py:537
  128.5 0.0 copy-start.2
  128.6 0.0 copy-start.1
  128.6 0.0 copy-start
  128.6 6.9 %convert_multiply_fusion = f32[8,128,2048]{2,1,0:T(8,128)} fusion(bf16[8,128,2048]{2,1,0:T(8,128)(2,1)} %get-tuple-element.11), kind=kLoop, calls=%fused_computation | loop fusion | flops 4194304 | bytes 12582912 | tf_op jit(solution)/shard_map/mul | solution.py:554
  135.5 0.0 copy-done.2
  135.5 1.0 copy.12
  136.5 0.0 copy-done.1
  136.5 1.0 copy.13
  137.5 0.0 copy-done
  137.5 1.0 copy.14
Async XLA Ops:
  128.5 7.0 %copy-start.2 = (bf16[512,1024]{1,0:T(8,128)(2,1)S(1)}, bf16[512,1024]{1,0:T(8,128)(2,1)}, u32[]{:S(2)}) copy-start(bf16[512,1024]{1,0:T(8,128)(2,1)} %get-tuple-element.16) | copy-start | bytes 3145732
  128.6 7.9 %copy-start.1 = (bf16[512,1024]{1,0:T(8,128)(2,1)S(1)}, bf16[512,1024]{1,0:T(8,128)(2,1)}, u32[]{:S(2)}) copy-start(bf16[512,1024]{1,0:T(8,128)(2,1)} %get-tuple-element.17) | copy-start | bytes 3145732
  128.6 8.9 %copy-start = (bf16[512,1024]{1,0:T(8,128)(2,1)S(1)}, bf16[512,1024]{1,0:T(8,128)(2,1)}, u32[]{:S(2)}) copy-start(bf16[512,1024]{1,0:T(8,128)(2,1)} %get-tuple-element.18) | copy-start | bytes 3145732

commit v2 on v1

v2 whole, which is shorter than its diff:
```python
import functools
import math

import jax
import jax.numpy as jnp
from jax import lax
from jax.experimental import pallas as pl
from jax.experimental.pallas import tpu as pltpu
from jax.sharding import PartitionSpec as P

HEADS = 8
WIDTH = 128
S1 = 16
ROWS = 512
PAIR = 256
CHIPS = 8
KEYS = 768
HALF = 384
FAR = 256
COLS = 2048
ALL = HEADS * WIDTH
UNITS = ((0, 3), (3, 3), (6, 2))
ORDERS = (
    (1, 0, 2), (0, 2, 1), (2, 1, 0), (1, 2, 0), (0, 1, 2), (2, 0, 1), (1, 0, 2), (1, 2, 0),
)
NSEM = 288
BF = jnp.bfloat16
F32 = jnp.float32
SCALE = 1.0 / math.sqrt(WIDTH)
EXP2_SCALE = math.log2(math.e) / math.sqrt(WIDTH)


def dot(a, b, ca, cb):
    return lax.dot_general(a, b, (((ca,), (cb,)), ((), ())), preferred_element_type=F32)


def flip4(a, d):
    if d == 0:
        return a
    if d == 1:
        return a + 1 - 2 * (a % 2)
    if d == 2:
        return (a + 2) % 4
    return 3 - a


def flip2(a, d):
    return 1 - a if d else a


class Place:
    def __init__(self):
        node = lax.axis_index("node")
        group = lax.axis_index("group")
        self.node, self.group = node, group
        self.core = node % 2
        self.z = (node // 2) % 4
        self.x_lo = node // 8
        self.x_hi = group // 4
        self.y = group % 4

    def coord(self, axis):
        return (self.x_hi * 2 + self.x_lo, self.y, self.z)[axis]

    def at(self, x_lo, x_hi, y, z, core):
        return {"node": (x_lo * 4 + z) * 2 + core, "group": x_hi * 4 + y}

    def sibling(self):
        return self.at(self.x_lo, self.x_hi, self.y, self.z, 1 - self.core)

    def chip(self, c):
        return self.at(
            flip2(self.x_lo, c // 4), self.x_hi, self.y, flip4(self.z, c % 4), self.core
        )

    def peer_group(self, j):
        return self.at(
            self.x_lo, flip2(self.x_hi, j // 4), flip4(self.y, j % 4), self.z, self.core
        )

    def coord_flip(self, axis, d):
        if axis == 0:
            return flip2(self.x_hi, d // 2) * 2 + flip2(self.x_lo, d % 2)
        return flip4(self.coord(axis), d)

    def along(self, axis, d):
        if axis == 0:
            return self.at(
                flip2(self.x_lo, d % 2), flip2(self.x_hi, d // 2), self.y, self.z, self.core
            )
        if axis == 1:
            return self.at(self.x_lo, self.x_hi, flip4(self.y, d), self.z, self.core)
        return self.at(self.x_lo, self.x_hi, self.y, flip4(self.z, d), self.core)


class Sems:
    def __init__(self, send_sems, recv_sems):
        self.send_sems, self.recv_sems, self.used = send_sems, recv_sems, 0

    def copy(self, src, dst, device):
        i = self.used
        self.used += 1
        return Copy(src, dst, self.send_sems.at[i], self.recv_sems.at[i], device)


class Copy:
    def __init__(self, src, dst, send_sem, recv_sem, device):
        self.parts = src, dst, send_sem, recv_sem, device

    def make(self):
        src, dst, send_sem, recv_sem, device = self.parts
        return pltpu.make_async_remote_copy(
            src_ref=src(),
            dst_ref=dst(),
            send_sem=send_sem,
            recv_sem=recv_sem,
            device_id=device(),
            device_id_type=pl.DeviceIdType.MESH,
        )

    def start(self):
        self.make().start()

    def wait(self):
        self.make().wait()


def start(copies):
    for copy in copies:
        copy.start()


def wait(copies):
    for copy in copies:
        copy.wait()


def kernel(
    q_hbm, k_hbm, v_hbm, go_hbm, w_hbm,
    gq_hbm, gk_hbm, gv_hbm, wout_hbm,
    q_ref, k_ref, v_ref, go_ref, w_ref,
    nf, zsend, zrecv, xblk, xsend, xrecv, gt, att, probs, gst, gs, delta,
    gnf, cr, snd, rr, yr, bxs, bxr, bzs, bzr, fine_k, fine_v, tot,
    wpart, wr0, ra, rb, rc, sa, sb, wout,
    load_sem, store_sem, send_sems, recv_sems,
):
    me = Place()
    core = me.core
    sems = Sems(send_sems, recv_sems)

    barrier = pltpu.get_barrier_semaphore()
    partners = [me.sibling()]
    partners += [me.chip(c) for c in range(1, CHIPS)]
    partners += [me.along(1, d) for d in range(1, 4)]
    partners += [me.along(0, d) for d in range(2, 4)]
    for partner in partners:
        pl.semaphore_signal(barrier, inc=1, device_id=partner, device_id_type=pl.DeviceIdType.MESH)

    loads = [
        pltpu.make_async_copy(src, dst, load_sem.at[i])
        for i, (src, dst) in enumerate(
            ((k_hbm, k_ref), (v_hbm, v_ref), (go_hbm, go_ref), (w_hbm, w_ref), (q_hbm, q_ref))
        )
    ]
    for load in loads:
        load.start()

    def near_at(c):
        return lambda: nf.at[:, pl.ds(32 * c, 32), :]

    def far_at(d):
        return lambda: nf.at[:, pl.ds(FAR + 32 * d, 32), :]

    def sib_at(first, rows):
        return lambda: nf.at[:, pl.ds(HALF + first, rows), :]

    z_gather = [
        sems.copy(lambda: zsend, lambda d=d: zrecv.at[d], lambda d=d: me.along(2, d))
        for d in range(1, 4)
    ]
    x_gather = [
        sems.copy(lambda: xsend, lambda d=d: xrecv.at[d], lambda d=d: me.along(0, d))
        for d in range(1, 4)
    ]
    y_gather = [
        sems.copy(far_at(0), far_at(d), lambda d=d: me.along(1, d)) for d in range(1, 4)
    ]
    near_gather = [
        sems.copy(near_at(0), near_at(c), lambda c=c: me.chip(c)) for c in range(1, CHIPS)
    ]
    near_forward = [
        sems.copy(near_at(c), sib_at(32 * c, 32), me.sibling) for c in range(CHIPS)
    ]
    far_forward = [
        sems.copy(far_at(d), sib_at(FAR + 32 * d, 32), me.sibling) for d in range(4)
    ]

    rows = lax.broadcasted_iota(jnp.int32, (32, ROWS), 0)
    toks = lax.broadcasted_iota(jnp.int32, (32, ROWS), 1)
    mean16 = jnp.where(toks // S1 == rows, 1.0 / S1, 0.0).astype(BF)
    r8 = lax.broadcasted_iota(jnp.int32, (8, 32), 0)
    c8 = lax.broadcasted_iota(jnp.int32, (8, 32), 1) // 16
    pick_k = jnp.where(c8 == r8, 1.0 / S1, 0.0).astype(BF)
    pick_v = jnp.where(c8 + 2 == r8, 1.0 / S1, 0.0).astype(BF)
    loads[0].wait()
    near_k = dot(mean16, k_ref[...], 1, 0).astype(BF)
    nf[0, 0:32, :] = near_k
    loads[1].wait()
    near_v = dot(mean16, v_ref[...], 1, 0).astype(BF)
    nf[1, 0:32, :] = near_v
    far_own = (dot(pick_k, near_k, 1, 0) + dot(pick_v, near_v, 1, 0)).astype(BF).astype(F32)
    zown = jnp.concatenate([far_own[0:4, 0 : ALL // 2], far_own[0:4, ALL // 2 :]], axis=0)
    zsend[...] = zown

    pl.semaphore_wait(barrier, len(partners))
    start(z_gather)
    start(near_gather)
    near_forward[0].start()

    def project(i, carry):
        r = pl.ds(pl.multiple_of(i * 256, 256), 256)
        gt[r, :] = dot(w_ref[r, :], go_ref[...], 1, 1).astype(BF)
        return carry

    loads[2].wait()
    loads[3].wait()
    lax.fori_loop(0, 2, project, 0)

    wait(z_gather)
    for d in range(4):
        block = zown if d == 0 else zrecv[d]
        for i in range(2):
            for part in range(2):
                xblk[8 * i + 2 * d : 8 * i + 2 * d + 2, part * 512 : part * 512 + 512] = block[
                    4 * part + 2 * i : 4 * part + 2 * i + 2
                ]
    xsend[...] = xblk[...].astype(BF)
    start(x_gather)
    lax.fori_loop(2, 4, project, 0)
    wait(x_gather)
    blocks = [xblk[...]] + [xrecv[d].astype(F32) for d in range(1, 4)]
    for i in range(2):
        nf[i, FAR : FAR + 32, :] = jnp.concatenate(
            [block[8 * i : 8 * i + 8] for block in blocks], axis=0
        ).astype(BF)
    start(y_gather)
    far_forward[0].start()
    loads[4].wait()
    for c in range(1, CHIPS):
        near_gather[c - 1].wait()
        near_forward[c].start()
    for d in range(1, 4):
        y_gather[d - 1].wait()
        far_forward[d].start()
    wait(near_forward)
    wait(far_forward)

    mine = pl.multiple_of(core * 64, 64)
    other = pl.multiple_of((1 - core) * 64, 64)

    def heads(u):
        return range(UNITS[u][0], UNITS[u][0] + UNITS[u][1])

    def span(u):
        return pl.ds(*UNITS[u])

    def columns(u):
        return pl.ds(UNITS[u][0] * WIDTH, UNITS[u][1] * WIDTH)

    def row_a(h, d=0):
        return pl.multiple_of(mine + me.coord_flip(ORDERS[h][0], d) * 16, 16)

    def col_b(h, d=0):
        return pl.multiple_of(me.coord_flip(ORDERS[h][1], d) * 512, 512)

    def col_c(h, d=0):
        return pl.multiple_of(me.coord_flip(ORDERS[h][2], d) * 128, 128)

    def piece(h, step):
        if step == 2:
            return wout.at[h, pl.ds(row_a(h), 16), pl.ds(col_b(h) + col_c(h), 128)]
        if step == 1:
            return wout.at[h, pl.ds(row_a(h), 16), pl.ds(col_b(h), 512)]
        return wout.at[h, pl.ds(row_a(h), 16), :]

    w_core, w_a, w_b, w_c, w_g, w_sib, w_out = [], [], [], [], [[], [], []], [], []
    for u in range(3):
        w_core.append(
            sems.copy(
                lambda u=u: wpart.at[span(u), pl.ds(other, 64), :],
                lambda u=u: wr0.at[span(u)],
                me.sibling,
            )
        )
        w_sib.append(
            sems.copy(
                lambda u=u: wout.at[span(u), pl.ds(mine, 64), :],
                lambda u=u: wout.at[span(u), pl.ds(mine, 64), :],
                me.sibling,
            )
        )
        w_out.append(
            pltpu.make_async_copy(wout.at[span(u)], wout_hbm.at[span(u)], store_sem.at[u])
        )
        w_a.append([
            sems.copy(
                lambda h=h, d=d: wpart.at[h, pl.ds(row_a(h, d), 16), :],
                lambda h=h, d=d: ra.at[d - 1, h],
                lambda h=h, d=d: me.along(ORDERS[h][0], d),
            )
            for h in heads(u) for d in range(1, 4)
        ])
        w_b.append([
            sems.copy(
                lambda h=h, d=d: sa.at[h, :, pl.ds(col_b(h, d), 512)],
                lambda h=h, d=d: rb.at[d - 1, h],
                lambda h=h, d=d: me.along(ORDERS[h][1], d),
            )
            for h in heads(u) for d in range(1, 4)
        ])
        w_c.append([
            sems.copy(
                lambda h=h, d=d: sb.at[h, :, pl.ds(col_c(h, d), 128)],
                lambda h=h, d=d: rc.at[d - 1, h],
                lambda h=h, d=d: me.along(ORDERS[h][2], d),
            )
            for h in heads(u) for d in range(1, 4)
        ])
        for step in range(3):
            w_g[step].append([
                sems.copy(
                    lambda h=h, step=step: piece(h, step),
                    lambda h=h, step=step: piece(h, step),
                    lambda h=h, d=d, step=step: me.along(ORDERS[h][step], d),
                )
                for h in heads(u) for d in range(1, 4)
            ])

    def weigh(u):
        def some(i, carry):
            c = pl.ds(pl.multiple_of(i * 512, 512), 512)
            part = dot(att[columns(u), :], go_ref[:, c], 1, 0)
            wpart[span(u), :, c] = part.reshape(UNITS[u][1], WIDTH, 512).astype(BF)
            return carry

        lax.fori_loop(0, COLS // 512, some, 0)
        w_core[u].start()

    def weight_core(u):
        w_core[u].wait()

        def some(h, carry):
            r = pl.ds(mine, 64)
            wpart[h, r, :] = (wpart[h, r, :].astype(F32) + wr0[h].astype(F32)).astype(BF)
            return carry

        lax.fori_loop(heads(u)[0], heads(u)[-1] + 1, some, 0)
        start(w_a[u])

    def weight_a(u):
        wait(w_a[u])
        for h in heads(u):
            t = wpart[h, pl.ds(row_a(h), 16), :].astype(F32)
            for d in range(3):
                t = t + ra[d, h].astype(F32)
            sa[h] = t.astype(BF)
        start(w_b[u])

    def weight_b(u):
        wait(w_b[u])
        for h in heads(u):
            t = sa[h, :, pl.ds(col_b(h), 512)].astype(F32)
            for d in range(3):
                t = t + rb[d, h].astype(F32)
            sb[h] = t.astype(BF)
        start(w_c[u])

    def weight_c(u):
        wait(w_c[u])
        for h in heads(u):
            t = sb[h, :, pl.ds(col_c(h), 128)].astype(F32)
            for d in range(3):
                t = t + rc[d, h].astype(F32)
            c = pl.multiple_of(col_b(h) + col_c(h), 128)
            wout[h, pl.ds(row_a(h), 16), pl.ds(c, 128)] = t.astype(BF)
        start(w_g[2][u])

    def weight_gather(u, step):
        wait(w_g[step][u])
        if step > 0:
            start(w_g[step - 1][u])
        else:
            w_sib[u].start()

    def weight_last(u):
        w_sib[u].wait()
        w_out[u].start()

    n_core, n_near, n_y, n_x, n_z = [], [], [], [], []
    for u in range(3):
        n_core.append(
            sems.copy(
                lambda u=u: gnf.at[:, pl.ds(HALF, HALF), columns(u)],
                lambda u=u: cr.at[:, :, columns(u)],
                me.sibling,
            )
        )
        n_near.append([
            sems.copy(
                lambda u=u, c=c: snd.at[:, pl.ds(32 * c, 32), columns(u)],
                lambda u=u, c=c: rr.at[c, :, :, columns(u)],
                lambda c=c: me.chip(c),
            )
            for c in range(1, CHIPS)
        ])
        n_y.append([
            sems.copy(
                lambda u=u, d=d: snd.at[:, pl.ds(FAR + 32 * d, 32), columns(u)],
                lambda u=u, d=d: yr.at[d, :, :, columns(u)],
                lambda d=d: me.along(1, d),
            )
            for d in range(1, 4)
        ])
        n_x.append([
            sems.copy(
                lambda u=u, d=d: bxs.at[d, :, columns(u)],
                lambda u=u, d=d: bxr.at[d, :, columns(u)],
                lambda d=d: me.along(0, d),
            )
            for d in range(1, 4)
        ])
        n_z.append([
            sems.copy(
                lambda u=u, d=d: bzs.at[d, :, columns(u)],
                lambda u=u, d=d: bzr.at[d, :, columns(u)],
                lambda d=d: me.along(2, d),
            )
            for d in range(1, 4)
        ])

    def near_core(u):
        n_core[u].wait()
        cs = columns(u)
        for i in range(2):
            snd[i, :, cs] = (gnf[i, 0:HALF, cs].astype(F32) + cr[i, :, cs].astype(F32)).astype(BF)
        start(n_near[u])
        start(n_y[u])

    def near_y(u):
        wait(n_y[u])
        cs = columns(u)
        sums = []
        for i in range(2):
            t = snd[i, FAR : FAR + 32, cs].astype(F32)
            for d in range(1, 4):
                t = t + yr[d, i, :, cs].astype(F32)
            sums.append(t)
        for d in range(4):
            r = slice(8 * d, 8 * d + 8)
            bxs[d, :, cs] = jnp.concatenate([sums[0][r], sums[1][r]], axis=0).astype(BF)
        start(n_x[u])

    def near_x(u):
        wait(n_x[u])
        cs = columns(u)
        t = bxs[0, :, cs].astype(F32)
        for d in range(1, 4):
            t = t + bxr[d, :, cs].astype(F32)
        for d in range(4):
            bzs[d, 0:2, cs] = t[2 * d : 2 * d + 2]
            bzs[d, 2:4, cs] = t[8 + 2 * d : 10 + 2 * d]
            bzs[d, 4:8, cs] = jnp.zeros((4, t.shape[1]), F32)
        start(n_z[u])

    def near_own(u):
        wait(n_near[u])
        cs = columns(u)
        for i in range(2):
            t = snd[i, 0:32, cs].astype(F32)
            for c in range(1, CHIPS):
                t = t + rr[c, i, :, cs].astype(F32)
            tot[i, :, cs] = t * (1.0 / S1)

    def near_z(u):
        wait(n_z[u])
        cs = columns(u)
        t = bzs[0, :, cs]
        for d in range(1, 4):
            t = t + bzr[d, :, cs]
        t = t * (1.0 / (S1 * S1))
        for i in range(2):
            for r in range(2):
                tot[i, 16 * r : 16 * r + 16, cs] = (
                    tot[i, 16 * r : 16 * r + 16, cs] + t[2 * i + r : 2 * i + r + 1]
                )

        def some(i, carry):
            r = pl.ds(pl.multiple_of(i * S1, S1), S1)
            k_ref[r, cs] = (fine_k[r, cs] + tot[0, pl.ds(i, 1), cs]).astype(BF)
            v_ref[r, cs] = (fine_v[r, cs] + tot[1, pl.ds(i, 1), cs]).astype(BF)
            return carry

        lax.fori_loop(0, ROWS // S1, some, 0, unroll=4)

    pair_row = lax.broadcasted_iota(jnp.int32, (32, ROWS), 0) // S1
    pair_col = lax.broadcasted_iota(jnp.int32, (32, ROWS), 1) // PAIR
    own_pair = pair_row == pair_col

    def forward(h):
        c = pl.ds(pl.multiple_of(h * WIDTH, WIDTH), WIDTH)
        qh = q_ref[:, c]
        s = dot(nf[0, :, c], qh, 1, 1)
        sf = [
            dot(k_ref[p * PAIR : (p + 1) * PAIR, c], qh[p * PAIR : (p + 1) * PAIR], 1, 1)
            for p in range(2)
        ]
        sf = jnp.concatenate(sf, axis=1)
        top = jnp.maximum(jnp.max(s, axis=0, keepdims=True), jnp.max(sf, axis=0, keepdims=True))
        e = jnp.exp2((s - top) * EXP2_SCALE)
        none = jnp.zeros((16, ROWS), F32)
        e = jnp.concatenate(
            [
                jnp.where(own_pair, 0.0, e[0:32]),
                e[32:FAR],
                none,
                e[FAR + 16 : HALF + FAR],
                none,
                e[HALF + FAR + 16 :],
            ],
            axis=0,
        )
        ef = jnp.exp2((sf - top) * EXP2_SCALE)
        total = jnp.sum(e, axis=0, keepdims=True) + jnp.sum(ef, axis=0, keepdims=True)
        e = e.astype(BF)
        ef = ef.astype(BF)
        probs[h, 0:KEYS, :] = e
        probs[h, KEYS : KEYS + PAIR, :] = ef
        out = dot(nf[1, :, c], e, 0, 0)
        of = [
            dot(v_ref[p * PAIR : (p + 1) * PAIR, c], ef[:, p * PAIR : (p + 1) * PAIR], 0, 0)
            for p in range(2)
        ]
        out = out + jnp.concatenate(of, axis=1)
        inv = 1.0 / total
        out = (out * inv).astype(BF)
        att[c, :] = out
        gth = gt[c, :].astype(F32)
        d = jnp.sum(out.astype(F32) * gth, axis=0, keepdims=True) * inv
        delta[h] = jnp.broadcast_to(d, (8, ROWS))
        scaled = gth * inv
        gst[c, :] = scaled.astype(BF)
        gs[:, c] = scaled.T.astype(BF)

    def backward(h):
        c = pl.ds(pl.multiple_of(h * WIDTH, WIDTH), WIDTH)
        qh = q_ref[:, c]
        gth = gst[c, :]
        gh = gs[:, c]
        d = delta[h, 0:1, :]
        e = probs[h, 0:KEYS, :]
        ds = (e.astype(F32) * (dot(nf[1, :, c], gth, 1, 0) - d)).astype(BF)
        gnf[1, :, c] = dot(e, gh, 1, 0).astype(BF)
        gnf[0, :, c] = (dot(ds, qh, 1, 0) * SCALE).astype(BF)
        dq = dot(nf[0, :, c], ds, 0, 0)
        dqf = []
        for p in range(2):
            r = slice(p * PAIR, (p + 1) * PAIR)
            ef = probs[h, KEYS : KEYS + PAIR, r]
            dsf = (ef.astype(F32) * (dot(v_ref[r, c], gth[:, r], 1, 0) - d[:, r])).astype(BF)
            fine_v[r, c] = dot(ef, gh[r], 1, 0)
            fine_k[r, c] = dot(dsf, qh[r], 1, 0) * SCALE
            dqf.append(dot(k_ref[r, c], dsf, 0, 0))
        dq = (dq + jnp.concatenate(dqf, axis=1)) * SCALE
        q_ref[:, c] = dq.T.astype(BF)

    def scheduled(work, plan):
        def step(h, carry):
            work(h)
            for at, actions in plan.items():

                @pl.when(h == at)
                def _():
                    for action, *args in actions:
                        action(*args)

            return carry

        lax.fori_loop(0, HEADS, step, 0)

    def near_send(u):
        n_core[u].start()

    scheduled(
        forward,
        {
            2: [(weigh, 0)],
            3: [(weight_core, 0)],
            5: [(weigh, 1)],
            6: [(weight_core, 1), (weight_a, 0)],
            7: [(weigh, 2), (weight_b, 0)],
        },
    )
    scheduled(
        backward,
        {
            0: [(weight_core, 2), (weight_c, 0), (weight_a, 1)],
            1: [(weight_gather, 0, 2), (weight_b, 1)],
            2: [(near_send, 0), (weight_gather, 0, 1), (weight_a, 2), (weight_c, 1)],
            3: [(near_core, 0), (weight_b, 2), (weight_gather, 1, 2)],
            4: [(weight_gather, 0, 0), (weight_c, 2), (weight_gather, 1, 1)],
            5: [(near_send, 1), (weight_last, 0), (weight_gather, 2, 2)],
            6: [(near_core, 1), (near_y, 0), (weight_gather, 2, 1)],
            7: [(near_send, 2), (near_x, 0), (weight_gather, 1, 0)],
        },
    )
    store_q = pltpu.make_async_copy(q_ref, gq_hbm, store_sem.at[3])
    store_q.start()
    near_core(2)
    near_y(1)
    near_own(0)
    near_z(0)
    weight_last(1)
    near_x(1)
    near_y(2)
    weight_gather(2, 0)
    near_own(1)
    near_z(1)
    near_x(2)
    weight_last(2)
    near_own(2)
    near_z(2)
    store_k = pltpu.make_async_copy(k_ref, gk_hbm, store_sem.at[4])
    store_v = pltpu.make_async_copy(v_ref, gv_hbm, store_sem.at[5])
    store_k.start()
    store_v.start()
    for copy in w_out + [store_q, store_k, store_v]:
        copy.wait()


def finish(
    scale, gq_in, gk_in, gv_in, w_in, gq_out, gk_out, gv_out, w_out, part, wide, in_sem, out_sem
):
    moves = [
        pltpu.make_async_copy(src, dst, in_sem.at[HEADS + i])
        for i, (src, dst) in enumerate(((gq_in, gq_out), (gk_in, gk_out), (gv_in, gv_out)))
    ]
    ins = [pltpu.make_async_copy(w_in.at[h], part.at[h], in_sem.at[h]) for h in range(HEADS)]
    outs = [
        pltpu.make_async_copy(wide.at[h], w_out.at[pl.ds(h * WIDTH, WIDTH)], out_sem.at[h])
        for h in range(HEADS)
    ]
    for copy in ins:
        copy.start()
    for copy in moves:
        copy.start()
    for h in range(HEADS):
        ins[h].wait()
        wide[h] = part[h].astype(F32) * scale
        outs[h].start()
    for copy in outs + moves:
        copy.wait()


def body(queries, key_rows, value_rows, grad_output, out_weight):
    vmem = pltpu.VMEM
    dma = pltpu.SemaphoreType.DMA
    scratch = [
        vmem((ROWS, ALL), BF),
        vmem((ROWS, ALL), BF),
        vmem((ROWS, ALL), BF),
        vmem((ROWS, COLS), BF),
        vmem((ALL, COLS), BF),
        vmem((2, KEYS, ALL), BF),
        vmem((8, ALL // 2), F32),
        vmem((4, 8, ALL // 2), F32),
        vmem((16, ALL), F32),
        vmem((16, ALL), BF),
        vmem((4, 16, ALL), BF),
        vmem((ALL, ROWS), BF),
        vmem((ALL, ROWS), BF),
        vmem((HEADS, KEYS + PAIR, ROWS), BF),
        vmem((ALL, ROWS), BF),
        vmem((ROWS, ALL), BF),
        vmem((HEADS, 8, ROWS), F32),
        vmem((2, KEYS, ALL), BF),
        vmem((2, HALF, ALL), BF),
        vmem((2, HALF, ALL), BF),
        vmem((CHIPS, 2, 32, ALL), BF),
        vmem((4, 2, 32, ALL), BF),
        vmem((4, 16, ALL), BF),
        vmem((4, 16, ALL), BF),
        vmem((4, 8, ALL), F32),
        vmem((4, 8, ALL), F32),
        vmem((ROWS, ALL), F32),
        vmem((ROWS, ALL), F32),
        vmem((2, 32, ALL), F32),
        vmem((HEADS, WIDTH, COLS), BF),
        vmem((HEADS, 64, COLS), BF),
        vmem((3, HEADS, 16, COLS), BF),
        vmem((3, HEADS, 16, 512), BF),
        vmem((3, HEADS, 16, 128), BF),
        vmem((HEADS, 16, COLS), BF),
        vmem((HEADS, 16, 512), BF),
        vmem((HEADS, WIDTH, COLS), BF),
        dma((5,)),
        dma((6,)),
        dma((NSEM,)),
        dma((NSEM,)),
    ]
    hbm = pl.BlockSpec(memory_space=pl.ANY)
    token_shape = jax.ShapeDtypeStruct((ROWS, ALL), BF)
    grads = pl.pallas_call(
        kernel,
        out_shape=(token_shape,) * 3 + (jax.ShapeDtypeStruct((HEADS, WIDTH, COLS), BF),),
        in_specs=[hbm] * 5,
        out_specs=(hbm,) * 4,
        scratch_shapes=scratch,
        compiler_params=pltpu.CompilerParams(
            collective_id=0, has_side_effects=True, vmem_limit_bytes=64 * 1024 * 1024 - 65536
        ),
        name="fused",
    )(queries, key_rows, value_rows, grad_output, out_weight)
    tokens = ROWS * lax.axis_size("node") * lax.axis_size("group")
    return pl.pallas_call(
        functools.partial(finish, 1.0 / math.sqrt(tokens)),
        out_shape=(token_shape,) * 3 + (jax.ShapeDtypeStruct((ALL, COLS), F32),),
        in_specs=[hbm] * 4,
        out_specs=(hbm,) * 4,
        scratch_shapes=[
            vmem((HEADS, WIDTH, COLS), BF),
            vmem((HEADS, WIDTH, COLS), F32),
            dma((HEADS + 3,)),
            dma((HEADS,)),
        ],
        compiler_params=pltpu.CompilerParams(vmem_limit_bytes=32 * 1024 * 1024),
        name="finish",
    )(*grads)


def solution(mesh):
    split = P(("group", "node"), None)
    return jax.shard_map(
        body,
        mesh=mesh,
        in_specs=(split, split, split, split, P()),
        out_specs=(split, split, split, P()),
        check_vma=False,
    )
```

time: 140 us -> 120 us (0.86)
  Pallas kernels: 128 us -> 113 us
  other arithmetic: 6.93 us -> 0 us
  local copies, waits for them, and re-layouts: 2.92 us -> 5.85 us
    pallas_call x1 -> x2, Pallas kernels: 128 us -> 113 us  [the longest x1 108 us: body(): pl.pallas_call(kernel, out_shape=(token_shape,) * 3 + (jax.ShapeDtypeStru...]
    mul x1 -> x0, other arithmetic: 6.93 us -> none  [body(): weight = weight.reshape(width, COLS).astype(F32) * (1.0 / math.sqrt(tokens))]
    unnamed x9 -> x8, local copies, waits for them, and re-layouts: 2.92 us -> 5.85 us
where the time goes in v2:
time: 120 us
  Pallas kernels  113 us (94%)
  local copies, waits for them, and re-layouts  5.85 us (5%)
    pallas_call x1, Pallas kernels, body(): pl.pallas_call(kernel, out_shape=(token_shape,) * 3 + (jax.ShapeDtypeStru...  108 us
    unnamed x8, local copies, waits for them, and re-layouts  5.85 us
    pallas_call x1, Pallas kernels, body(): pl.pallas_call(functools.partial(finish, 1.0 / math.sqrt(tokens)), out_sh...  4.7 us

profile of v2, /device:TPU:0, one launch (start us, length us, event | category | flops | bytes accessed | tf_op | source)
XLA Modules:
  0.0 119.7 jit_solution(4746706426288433831)
XLA Ops:
  0.6 108.5 %fused.1 = (bf16[512,1024]{1,0:T(8,128)(2,1)}, bf16[512,1024]{1,0:T(8,128)(2,1)}, bf16[512,1024]{1,0:T(8,128)(2,1)}, bf16[8,128,2048]{2,1,0:T(8,128)(2,1)}) custom-call(bf16[512,1024]{1,0:T(8,128)(2,1)} %q_hbm.1, bf16[512,1024]{1,0:T(8,128)(2,1)} %k_hbm.1, bf16[512,1024]{1,0:T(8,128)(2,1)} %v_hbm.1, bf16[512,2048]{1,0:T(8,128)(2,1)} %go_hbm.1, ...), custom_call_target="tpu_custom_call" | custom-call | tf_op jit(solution)/shard_map/fused/pallas_call | solution.py:712
  109.1 0.0 copy-start
  109.1 2.2 %copy-done = bf16[8,128,2048]{2,1,0:T(8,128)(2,1)S(1)} copy-done((bf16[8,128,2048]{2,1,0:T(8,128)(2,1)S(1)}, bf16[8,128,2048]{2,1,0:T(8,128)(2,1)}, u32[]{:S(2)}) %copy-start) | copy-done | bytes 4194328
  111.3 0.0 copy-start.1
  111.3 1.2 %copy-done.1 = bf16[512,1024]{1,0:T(8,128)(2,1)S(1)} copy-done((bf16[512,1024]{1,0:T(8,128)(2,1)S(1)}, bf16[512,1024]{1,0:T(8,128)(2,1)}, u32[]{:S(2)}) %copy-start.1) | copy-done | bytes 1048600
  112.5 0.0 copy-start.2
  112.5 1.2 %copy-done.2 = bf16[512,1024]{1,0:T(8,128)(2,1)S(1)} copy-done((bf16[512,1024]{1,0:T(8,128)(2,1)S(1)}, bf16[512,1024]{1,0:T(8,128)(2,1)}, u32[]{:S(2)}) %copy-start.2) | copy-done | bytes 1048600
  113.8 0.0 copy-start.3
  113.8 1.2 %copy-done.3 = bf16[512,1024]{1,0:T(8,128)(2,1)S(1)} copy-done((bf16[512,1024]{1,0:T(8,128)(2,1)S(1)}, bf16[512,1024]{1,0:T(8,128)(2,1)}, u32[]{:S(2)}) %copy-start.3) | copy-done | bytes 1048600
  115.0 4.7 %finish.1 = (bf16[512,1024]{1,0:T(8,128)(2,1)}, bf16[512,1024]{1,0:T(8,128)(2,1)}, bf16[512,1024]{1,0:T(8,128)(2,1)}, f32[1024,2048]{1,0:T(8,128)}) custom-call(bf16[512,1024]{1,0:T(8,128)(2,1)S(1)} %copy-done.1, bf16[512,1024]{1,0:T(8,128)(2,1)S(1)} %copy-done.2, bf16[512,1024]{1,0:T(8,128)(2,1)S(1)} %copy-done.3, bf16[8,128,2048]{2,1,0:T(8,128)(2,1)S(1)} %copy-done), custom_call_target="tpu_custom_call" | custom-call | tf_op jit(solution)/shard_map/finish/pallas_call | solution.py:724
Async XLA Ops:
  109.1 2.2 %copy-start = (bf16[8,128,2048]{2,1,0:T(8,128)(2,1)S(1)}, bf16[8,128,2048]{2,1,0:T(8,128)(2,1)}, u32[]{:S(2)}) copy-start(bf16[8,128,2048]{2,1,0:T(8,128)(2,1)} %get-tuple-element.11.w_in) | copy-start | bytes 12582916
  111.3 1.2 %copy-start.1 = (bf16[512,1024]{1,0:T(8,128)(2,1)S(1)}, bf16[512,1024]{1,0:T(8,128)(2,1)}, u32[]{:S(2)}) copy-start(bf16[512,1024]{1,0:T(8,128)(2,1)} %get-tuple-element.8.gq_in) | copy-start | bytes 3145732
  112.5 1.2 %copy-start.2 = (bf16[512,1024]{1,0:T(8,128)(2,1)S(1)}, bf16[512,1024]{1,0:T(8,128)(2,1)}, u32[]{:S(2)}) copy-start(bf16[512,1024]{1,0:T(8,128)(2,1)} %get-tuple-element.9.gk_in) | copy-start | bytes 3145732
  113.8 1.2 %copy-start.3 = (bf16[512,1024]{1,0:T(8,128)(2,1)S(1)}, bf16[512,1024]{1,0:T(8,128)(2,1)}, u32[]{:S(2)}) copy-start(bf16[512,1024]{1,0:T(8,128)(2,1)} %get-tuple-element.10.gv_in) | copy-start | bytes 3145732

commit v3 on v2

--- a/solution.py
+++ b/solution.py
@@ -21,9 +21,9 @@
 ALL = HEADS * WIDTH
 UNITS = ((0, 3), (3, 3), (6, 2))
 ORDERS = (
-    (1, 0, 2), (0, 2, 1), (2, 1, 0), (1, 2, 0), (0, 1, 2), (2, 0, 1), (1, 0, 2), (1, 2, 0),
+    (1, 0, 2), (0, 1, 2), (2, 0, 1), (1, 0, 2), (0, 1, 2), (2, 1, 0), (1, 2, 0), (0, 2, 1),
 )
-NSEM = 288
+NSEM = 232
 BF = jnp.bfloat16
 F32 = jnp.float32
 SCALE = 1.0 / math.sqrt(WIDTH)
@@ -52,45 +52,35 @@
     def __init__(self):
         node = lax.axis_index("node")
         group = lax.axis_index("group")
-        self.node, self.group = node, group
         self.core = node % 2
-        self.z = (node // 2) % 4
-        self.x_lo = node // 8
-        self.x_hi = group // 4
-        self.y = group % 4
-
-    def coord(self, axis):
-        return (self.x_hi * 2 + self.x_lo, self.y, self.z)[axis]
-
-    def at(self, x_lo, x_hi, y, z, core):
-        return {"node": (x_lo * 4 + z) * 2 + core, "group": x_hi * 4 + y}
+        z = (node // 2) % 4
+        x_lo = node // 8
+        x_hi = group // 4
+        y = group % 4
+        los, his = [flip2(x_lo, d) for d in range(2)], [flip2(x_hi, d) for d in range(2)]
+        zs, ys = [flip4(z, d) for d in range(4)], [flip4(y, d) for d in range(4)]
+        self.flips = [[his[d // 2] * 2 + los[d % 2] for d in range(4)], ys, zs]
+        self.sib = {"node": node + 1 - 2 * self.core, "group": group}
+        self.crosses = [
+            {"node": (los[m // 4 % 2] * 4 + zs[m % 4]) * 2 + self.core, "group": his[m // 8] * 4 + y}
+            for m in range(16)
+        ]
+        self.ys = [{"node": node, "group": x_hi * 4 + ys[d]} for d in range(4)]
+
+    def coord_flip(self, axis, d):
+        return self.flips[axis][d]
 
     def sibling(self):
-        return self.at(self.x_lo, self.x_hi, self.y, self.z, 1 - self.core)
+        return self.sib
+
+    def cross(self, m):
+        return self.crosses[m]
 
     def chip(self, c):
-        return self.at(
-            flip2(self.x_lo, c // 4), self.x_hi, self.y, flip4(self.z, c % 4), self.core
-        )
-
-    def peer_group(self, j):
-        return self.at(
-            self.x_lo, flip2(self.x_hi, j // 4), flip4(self.y, j % 4), self.z, self.core
-        )
-
-    def coord_flip(self, axis, d):
-        if axis == 0:
-            return flip2(self.x_hi, d // 2) * 2 + flip2(self.x_lo, d % 2)
-        return flip4(self.coord(axis), d)
+        return self.crosses[c]
 
     def along(self, axis, d):
-        if axis == 0:
-            return self.at(
-                flip2(self.x_lo, d % 2), flip2(self.x_hi, d // 2), self.y, self.z, self.core
-            )
-        if axis == 1:
-            return self.at(self.x_lo, self.x_hi, flip4(self.y, d), self.z, self.core)
-        return self.at(self.x_lo, self.x_hi, self.y, flip4(self.z, d), self.core)
+        return (self.crosses[4 * d], self.ys[d], self.crosses[d])[axis]
 
 
 class Sems:
@@ -139,8 +129,8 @@
     q_hbm, k_hbm, v_hbm, go_hbm, w_hbm,
     gq_hbm, gk_hbm, gv_hbm, wout_hbm,
     q_ref, k_ref, v_ref, go_ref, w_ref,
-    nf, zsend, zrecv, xblk, xsend, xrecv, gt, att, probs, gst, gs, delta,
-    gnf, cr, snd, rr, yr, bxs, bxr, bzs, bzr, fine_k, fine_v, tot,
+    nf, zsend, zrecv, xblk, gt, att, probs, gst, gs, delta,
+    gnf, cr, near_snd, far_snd, zr, xs, xr, yr, packed, bxs, bxr, fine_k, fine_v, tot,
     wpart, wr0, ra, rb, rc, sa, sb, wout,
     load_sem, store_sem, send_sems, recv_sems,
 ):
@@ -150,9 +140,8 @@
 
     barrier = pltpu.get_barrier_semaphore()
     partners = [me.sibling()]
-    partners += [me.chip(c) for c in range(1, CHIPS)]
+    partners += [me.cross(m) for m in range(1, 16)]
     partners += [me.along(1, d) for d in range(1, 4)]
-    partners += [me.along(0, d) for d in range(2, 4)]
     for partner in partners:
         pl.semaphore_signal(barrier, inc=1, device_id=partner, device_id_type=pl.DeviceIdType.MESH)
 
@@ -174,13 +163,9 @@
     def sib_at(first, rows):
         return lambda: nf.at[:, pl.ds(HALF + first, rows), :]
 
-    z_gather = [
-        sems.copy(lambda: zsend, lambda d=d: zrecv.at[d], lambda d=d: me.along(2, d))
-        for d in range(1, 4)
-    ]
-    x_gather = [
-        sems.copy(lambda: xsend, lambda d=d: xrecv.at[d], lambda d=d: me.along(0, d))
-        for d in range(1, 4)
+    own_gather = [
+        sems.copy(lambda: zsend, lambda m=m: zrecv.at[m], lambda m=m: me.cross(m))
+        for m in range(1, 16)
     ]
     y_gather = [
         sems.copy(far_at(0), far_at(d), lambda d=d: me.along(1, d)) for d in range(1, 4)
@@ -209,11 +194,12 @@
     near_v = dot(mean16, v_ref[...], 1, 0).astype(BF)
     nf[1, 0:32, :] = near_v
     far_own = (dot(pick_k, near_k, 1, 0) + dot(pick_v, near_v, 1, 0)).astype(BF).astype(F32)
-    zown = jnp.concatenate([far_own[0:4, 0 : ALL // 2], far_own[0:4, ALL // 2 :]], axis=0)
-    zsend[...] = zown
+    zsend[...] = jnp.concatenate(
+        [far_own[0:4, 256 * part : 256 * part + 256] for part in range(4)], axis=0
+    ).astype(BF)
 
     pl.semaphore_wait(barrier, len(partners))
-    start(z_gather)
+    start(own_gather)
     start(near_gather)
     near_forward[0].start()
 
@@ -224,25 +210,17 @@
 
     loads[2].wait()
     loads[3].wait()
-    lax.fori_loop(0, 2, project, 0)
-
-    wait(z_gather)
-    for d in range(4):
-        block = zown if d == 0 else zrecv[d]
+    lax.fori_loop(0, 4, project, 0)
+
+    wait(own_gather)
+    for m in range(16):
+        block = (zsend[...] if m == 0 else zrecv[m]).astype(F32)
         for i in range(2):
-            for part in range(2):
-                xblk[8 * i + 2 * d : 8 * i + 2 * d + 2, part * 512 : part * 512 + 512] = block[
+            for part in range(4):
+                xblk[i, 2 * m : 2 * m + 2, part * 256 : part * 256 + 256] = block[
                     4 * part + 2 * i : 4 * part + 2 * i + 2
                 ]
-    xsend[...] = xblk[...].astype(BF)
-    start(x_gather)
-    lax.fori_loop(2, 4, project, 0)
-    wait(x_gather)
-    blocks = [xblk[...]] + [xrecv[d].astype(F32) for d in range(1, 4)]
-    for i in range(2):
-        nf[i, FAR : FAR + 32, :] = jnp.concatenate(
-            [block[8 * i : 8 * i + 8] for block in blocks], axis=0
-        ).astype(BF)
+    nf[:, FAR : FAR + 32, :] = xblk[...].astype(BF)
     start(y_gather)
     far_forward[0].start()
     loads[4].wait()
@@ -267,18 +245,32 @@
     def columns(u):
         return pl.ds(UNITS[u][0] * WIDTH, UNITS[u][1] * WIDTH)
 
+    def offsets(unit, first=0):
+        return [
+            [pl.multiple_of(first + me.coord_flip(axis, d) * unit, unit) for d in range(4)]
+            for axis in range(3)
+        ]
+
+    rows_a, cols_b, cols_c = offsets(16, mine), offsets(512), offsets(128)
+    cols_bc = [
+        [pl.multiple_of(cols_b[b][0] + cols_c[c][0], 128) for c in range(3)] for b in range(3)
+    ]
+
     def row_a(h, d=0):
-        return pl.multiple_of(mine + me.coord_flip(ORDERS[h][0], d) * 16, 16)
+        return rows_a[ORDERS[h][0]][d]
 
     def col_b(h, d=0):
-        return pl.multiple_of(me.coord_flip(ORDERS[h][1], d) * 512, 512)
+        return cols_b[ORDERS[h][1]][d]
 
     def col_c(h, d=0):
-        return pl.multiple_of(me.coord_flip(ORDERS[h][2], d) * 128, 128)
+        return cols_c[ORDERS[h][2]][d]
+
+    def col_bc(h):
+        return cols_bc[ORDERS[h][1]][ORDERS[h][2]]
 
     def piece(h, step):
         if step == 2:
-            return wout.at[h, pl.ds(row_a(h), 16), pl.ds(col_b(h) + col_c(h), 128)]
+            return wout.at[h, pl.ds(row_a(h), 16), pl.ds(col_bc(h), 128)]
         if step == 1:
             return wout.at[h, pl.ds(row_a(h), 16), pl.ds(col_b(h), 512)]
         return wout.at[h, pl.ds(row_a(h), 16), :]
@@ -381,8 +373,7 @@
             t = sb[h, :, pl.ds(col_c(h), 128)].astype(F32)
             for d in range(3):
                 t = t + rc[d, h].astype(F32)
-            c = pl.multiple_of(col_b(h) + col_c(h), 128)
-            wout[h, pl.ds(row_a(h), 16), pl.ds(c, 128)] = t.astype(BF)
+            wout[h, pl.ds(row_a(h), 16), pl.ds(col_bc(h), 128)] = t.astype(BF)
         start(w_g[2][u])
 
     def weight_gather(u, step):
@@ -396,7 +387,7 @@
         w_sib[u].wait()
         w_out[u].start()
 
-    n_core, n_near, n_y, n_x, n_z = [], [], [], [], []
+    n_core, n_z, n_x, n_y = [], [], [], []
     for u in range(3):
         n_core.append(
             sems.copy(
@@ -405,102 +396,103 @@
                 me.sibling,
             )
         )
-        n_near.append([
-            sems.copy(
-                lambda u=u, c=c: snd.at[:, pl.ds(32 * c, 32), columns(u)],
-                lambda u=u, c=c: rr.at[c, :, :, columns(u)],
-                lambda c=c: me.chip(c),
-            )
-            for c in range(1, CHIPS)
+        n_z.append([
+            sems.copy(
+                lambda u=u, d=d: near_snd.at[:, :, d, :, columns(u)],
+                lambda u=u, d=d: zr.at[d, :, :, :, columns(u)],
+                lambda d=d: me.along(2, d),
+            )
+            for d in range(1, 4)
         ])
+        n_x.append(
+            sems.copy(
+                lambda u=u: xs.at[:, :, columns(u)],
+                lambda u=u: xr.at[:, :, columns(u)],
+                lambda: me.chip(4),
+            )
+        )
         n_y.append([
             sems.copy(
-                lambda u=u, d=d: snd.at[:, pl.ds(FAR + 32 * d, 32), columns(u)],
+                lambda u=u, d=d: far_snd.at[:, pl.ds(32 * d, 32), columns(u)],
                 lambda u=u, d=d: yr.at[d, :, :, columns(u)],
                 lambda d=d: me.along(1, d),
             )
             for d in range(1, 4)
         ])
-        n_x.append([
-            sems.copy(
-                lambda u=u, d=d: bxs.at[d, :, columns(u)],
-                lambda u=u, d=d: bxr.at[d, :, columns(u)],
-                lambda d=d: me.along(0, d),
-            )
-            for d in range(1, 4)
-        ])
-        n_z.append([
-            sems.copy(
-                lambda u=u, d=d: bzs.at[d, :, columns(u)],
-                lambda u=u, d=d: bzr.at[d, :, columns(u)],
-                lambda d=d: me.along(2, d),
-            )
-            for d in range(1, 4)
-        ])
+    own_reduce = [
+        sems.copy(lambda m=m: bxs.at[m], lambda m=m: bxr.at[m], lambda m=m: me.cross(m))
+        for m in range(1, 16)
+    ]
 
     def near_core(u):
         n_core[u].wait()
         cs = columns(u)
         for i in range(2):
-            snd[i, :, cs] = (gnf[i, 0:HALF, cs].astype(F32) + cr[i, :, cs].astype(F32)).astype(BF)
-        start(n_near[u])
+            t = (gnf[i, 0:HALF, cs].astype(F32) + cr[i, :, cs].astype(F32)).astype(BF)
+            for c in range(CHIPS):
+                near_snd[i, c // 4, c % 4, :, cs] = t[32 * c : 32 * c + 32]
+            far_snd[i, :, cs] = t[FAR:]
+        start(n_z[u])
         start(n_y[u])
+
+    def near_z(u):
+        wait(n_z[u])
+        cs = columns(u)
+        for i in range(2):
+            for x in range(2):
+                t = near_snd[i, x, 0, :, cs].astype(F32)
+                for d in range(1, 4):
+                    t = t + zr[d, i, x, :, cs].astype(F32)
+                if x == 0:
+                    tot[i, :, cs] = t
+                else:
+                    xs[i, :, cs] = t.astype(BF)
+        n_x[u].start()
+
+    def near_x(u):
+        n_x[u].wait()
+        cs = columns(u)
+        for i in range(2):
+            tot[i, :, cs] = (tot[i, :, cs] + xr[i, :, cs].astype(F32)) * (1.0 / S1)
 
     def near_y(u):
         wait(n_y[u])
         cs = columns(u)
-        sums = []
         for i in range(2):
-            t = snd[i, FAR : FAR + 32, cs].astype(F32)
+            t = far_snd[i, 0:32, cs].astype(F32)
             for d in range(1, 4):
                 t = t + yr[d, i, :, cs].astype(F32)
-            sums.append(t)
-        for d in range(4):
-            r = slice(8 * d, 8 * d + 8)
-            bxs[d, :, cs] = jnp.concatenate([sums[0][r], sums[1][r]], axis=0).astype(BF)
-        start(n_x[u])
-
-    def near_x(u):
-        wait(n_x[u])
-        cs = columns(u)
-        t = bxs[0, :, cs].astype(F32)
-        for d in range(1, 4):
-            t = t + bxr[d, :, cs].astype(F32)
-        for d in range(4):
-            bzs[d, 0:2, cs] = t[2 * d : 2 * d + 2]
-            bzs[d, 2:4, cs] = t[8 + 2 * d : 10 + 2 * d]
-            bzs[d, 4:8, cs] = jnp.zeros((4, t.shape[1]), F32)
-        start(n_z[u])
-
-    def near_own(u):
-        wait(n_near[u])
-        cs = columns(u)
-        for i in range(2):
-            t = snd[i, 0:32, cs].astype(F32)
-            for c in range(1, CHIPS):
-                t = t + rr[c, i, :, cs].astype(F32)
-            tot[i, :, cs] = t * (1.0 / S1)
-
-    def near_z(u):
-        wait(n_z[u])
-        cs = columns(u)
-        t = bzs[0, :, cs]
-        for d in range(1, 4):
-            t = t + bzr[d, :, cs]
+            xblk[i, :, cs] = t
+        for part in ((), (0, 1, 2), (3,))[u]:
+            for m in range(16):
+                for i in range(2):
+                    packed[m, 4 * part + 2 * i : 4 * part + 2 * i + 2, :] = xblk[
+                        i, 2 * m : 2 * m + 2, part * 256 : part * 256 + 256
+                    ]
+        if u == 2:
+            bxs[...] = packed[...].astype(BF)
+            start(own_reduce)
+
+    def finish_rows():
+        wait(own_reduce)
+        t = bxs[0].astype(F32)
+        for m in range(1, 16):
+            t = t + bxr[m].astype(F32)
         t = t * (1.0 / (S1 * S1))
         for i in range(2):
             for r in range(2):
-                tot[i, 16 * r : 16 * r + 16, cs] = (
-                    tot[i, 16 * r : 16 * r + 16, cs] + t[2 * i + r : 2 * i + r + 1]
+                far_row = jnp.concatenate(
+                    [t[4 * p + 2 * i + r : 4 * p + 2 * i + r + 1] for p in range(4)], axis=1
                 )
+                tot[i, 16 * r : 16 * r + 16, :] = tot[i, 16 * r : 16 * r + 16, :] + far_row
 
         def some(i, carry):
             r = pl.ds(pl.multiple_of(i * S1, S1), S1)
-            k_ref[r, cs] = (fine_k[r, cs] + tot[0, pl.ds(i, 1), cs]).astype(BF)
-            v_ref[r, cs] = (fine_v[r, cs] + tot[1, pl.ds(i, 1), cs]).astype(BF)
+            k_ref[r, :] = (fine_k[r, :] + tot[0, pl.ds(i, 1), :]).astype(BF)
+            v_ref[r, :] = (fine_v[r, :] + tot[1, pl.ds(i, 1), :]).astype(BF)
             return carry
 
-        lax.fori_loop(0, ROWS // S1, some, 0, unroll=4)
+        lax.fori_loop(0, ROWS // S1, some, 0, unroll=2)
 
     pair_row = lax.broadcasted_iota(jnp.int32, (32, ROWS), 0) // S1
     pair_col = lax.broadcasted_iota(jnp.int32, (32, ROWS), 1) // PAIR
@@ -596,68 +588,77 @@
             2: [(weigh, 0)],
             3: [(weight_core, 0)],
             5: [(weigh, 1)],
-            6: [(weight_core, 1), (weight_a, 0)],
-            7: [(weigh, 2), (weight_b, 0)],
+            6: [(weight_core, 1)],
+            7: [(weight_a, 0), (weigh, 2)],
         },
     )
     scheduled(
         backward,
         {
-            0: [(weight_core, 2), (weight_c, 0), (weight_a, 1)],
-            1: [(weight_gather, 0, 2), (weight_b, 1)],
-            2: [(near_send, 0), (weight_gather, 0, 1), (weight_a, 2), (weight_c, 1)],
-            3: [(near_core, 0), (weight_b, 2), (weight_gather, 1, 2)],
-            4: [(weight_gather, 0, 0), (weight_c, 2), (weight_gather, 1, 1)],
-            5: [(near_send, 1), (weight_last, 0), (weight_gather, 2, 2)],
-            6: [(near_core, 1), (near_y, 0), (weight_gather, 2, 1)],
-            7: [(near_send, 2), (near_x, 0), (weight_gather, 1, 0)],
+            0: [(weight_core, 2)],
+            1: [(weight_a, 1)],
+            2: [(near_send, 0), (weight_b, 0)],
+            3: [(near_core, 0)],
+            4: [(weight_a, 2), (weight_b, 1)],
+            5: [(near_send, 1), (weight_c, 0)],
+            6: [(near_core, 1), (weight_c, 1)],
+            7: [(near_send, 2), (weight_b, 2), (weight_gather, 0, 2), (near_z, 0)],
         },
     )
     store_q = pltpu.make_async_copy(q_ref, gq_hbm, store_sem.at[3])
     store_q.start()
     near_core(2)
+    weight_gather(1, 2)
+    near_y(0)
+    weight_c(2)
+    weight_gather(0, 1)
+    near_z(1)
     near_y(1)
-    near_own(0)
-    near_z(0)
+    weight_gather(1, 1)
+    near_y(2)
+    weight_gather(2, 2)
+    near_z(2)
+    weight_gather(0, 0)
+    weight_gather(1, 0)
+    near_x(0)
+    near_x(1)
+    weight_gather(2, 1)
+    weight_last(0)
     weight_last(1)
-    near_x(1)
-    near_y(2)
-    weight_gather(2, 0)
-    near_own(1)
-    near_z(1)
     near_x(2)
-    weight_last(2)
-    near_own(2)
-    near_z(2)
+    finish_rows()
     store_k = pltpu.make_async_copy(k_ref, gk_hbm, store_sem.at[4])
     store_v = pltpu.make_async_copy(v_ref, gv_hbm, store_sem.at[5])
     store_k.start()
     store_v.start()
+    weight_gather(2, 0)
+    weight_last(2)
     for copy in w_out + [store_q, store_k, store_v]:
         copy.wait()
 
 
 def finish(
-    scale, gq_in, gk_in, gv_in, w_in, gq_out, gk_out, gv_out, w_out, part, wide, in_sem, out_sem
+    scale, gq_in, gk_in, gv_in, w_in, gq_out, gk_out, gv_out, w_out,
+    part, wide, kept, in_sem, out_sem,
 ):
-    moves = [
-        pltpu.make_async_copy(src, dst, in_sem.at[HEADS + i])
-        for i, (src, dst) in enumerate(((gq_in, gq_out), (gk_in, gk_out), (gv_in, gv_out)))
-    ]
     ins = [pltpu.make_async_copy(w_in.at[h], part.at[h], in_sem.at[h]) for h in range(HEADS)]
     outs = [
         pltpu.make_async_copy(wide.at[h], w_out.at[pl.ds(h * WIDTH, WIDTH)], out_sem.at[h])
         for h in range(HEADS)
     ]
+    for i, (src, dst) in enumerate(((gq_in, gq_out), (gk_in, gk_out), (gv_in, gv_out))):
+        ins.append(pltpu.make_async_copy(src, kept.at[i], in_sem.at[HEADS + i]))
+        outs.append(pltpu.make_async_copy(kept.at[i], dst, out_sem.at[HEADS + i]))
     for copy in ins:
-        copy.start()
-    for copy in moves:
         copy.start()
     for h in range(HEADS):
         ins[h].wait()
         wide[h] = part[h].astype(F32) * scale
         outs[h].start()
-    for copy in outs + moves:
+    for i in range(HEADS, HEADS + 3):
+        ins[i].wait()
+        outs[i].start()
+    for copy in outs:
         copy.wait()
 
 
@@ -671,11 +672,9 @@
         vmem((ROWS, COLS), BF),
         vmem((ALL, COLS), BF),
         vmem((2, KEYS, ALL), BF),
-        vmem((8, ALL // 2), F32),
-        vmem((4, 8, ALL // 2), F32),
-        vmem((16, ALL), F32),
-        vmem((16, ALL), BF),
-        vmem((4, 16, ALL), BF),
+        vmem((16, 256), BF),
+        vmem((16, 16, 256), BF),
+        vmem((2, 32, ALL), F32),
         vmem((ALL, ROWS), BF),
         vmem((ALL, ROWS), BF),
         vmem((HEADS, KEYS + PAIR, ROWS), BF),
@@ -684,13 +683,15 @@
         vmem((HEADS, 8, ROWS), F32),
         vmem((2, KEYS, ALL), BF),
         vmem((2, HALF, ALL), BF),
-        vmem((2, HALF, ALL), BF),
-        vmem((CHIPS, 2, 32, ALL), BF),
+        vmem((2, 2, 4, 32, ALL), BF),
+        vmem((2, 128, ALL), BF),
+        vmem((4, 2, 2, 32, ALL), BF),
+        vmem((2, 32, ALL), BF),
+        vmem((2, 32, ALL), BF),
         vmem((4, 2, 32, ALL), BF),
-        vmem((4, 16, ALL), BF),
-        vmem((4, 16, ALL), BF),
-        vmem((4, 8, ALL), F32),
-        vmem((4, 8, ALL), F32),
+        vmem((16, 16, 256), F32),
+        vmem((16, 16, 256), BF),
+        vmem((16, 16, 256), BF),
         vmem((ROWS, ALL), F32),
         vmem((ROWS, ALL), F32),
         vmem((2, 32, ALL), F32),
@@ -729,10 +730,11 @@
         scratch_shapes=[
             vmem((HEADS, WIDTH, COLS), BF),
             vmem((HEADS, WIDTH, COLS), F32),
+            vmem((3, ROWS, ALL), BF),
             dma((HEADS + 3,)),
-            dma((HEADS,)),
+            dma((HEADS + 3,)),
         ],
-        compiler_params=pltpu.CompilerParams(vmem_limit_bytes=32 * 1024 * 1024),
+        compiler_params=pltpu.CompilerParams(vmem_limit_bytes=64 * 1024 * 1024 - 65536),
         name="finish",
     )(*grads)
 

time: 120 us -> 98.2 us (0.82)
  Pallas kernels: 113 us -> 96.2 us
  local copies, waits for them, and re-layouts: 5.85 us -> 0 us
    pallas_call x1, Pallas kernels: 108 us -> 89.3 us  [body(): pl.pallas_call(kernel, out_shape=(token_shape,) * 3 + (jax.ShapeDtypeStru...]
    unnamed x8 -> x0, local copies, waits for them, and re-layouts: 5.85 us -> none
    pallas_call x1, Pallas kernels: 4.7 us -> 6.81 us  [body(): pl.pallas_call(functools.partial(finish, 1.0 / math.sqrt(tokens)), out_sh...]
where the time goes in v3:
time: 98.2 us; the launch traced here: 96.8 us
  Pallas kernels  96.2 us (98%)
    pallas_call x1, Pallas kernels, body(): pl.pallas_call(kernel, out_shape=(token_shape,) * 3 + (jax.ShapeDtypeStru...  89.3 us
    pallas_call x1, Pallas kernels, body(): pl.pallas_call(functools.partial(finish, 1.0 / math.sqrt(tokens)), out_sh...  6.81 us

profile of v3, /device:TPU:0, one launch (start us, length us, event | category | flops | bytes accessed | tf_op | source)
XLA Modules:
  0.0 96.8 jit_solution(13165727457107678862)
XLA Ops:
  0.6 89.3 %fused.1 = (bf16[512,1024]{1,0:T(8,128)(2,1)}, bf16[512,1024]{1,0:T(8,128)(2,1)}, bf16[512,1024]{1,0:T(8,128)(2,1)}, bf16[8,128,2048]{2,1,0:T(8,128)(2,1)}) custom-call(bf16[512,1024]{1,0:T(8,128)(2,1)} %q_hbm.1, bf16[512,1024]{1,0:T(8,128)(2,1)} %k_hbm.1, bf16[512,1024]{1,0:T(8,128)(2,1)} %v_hbm.1, bf16[512,2048]{1,0:T(8,128)(2,1)} %go_hbm.1, ...), custom_call_target="tpu_custom_call" | custom-call | tf_op jit(solution)/shard_map/fused/pallas_call | solution.py:713
  90.0 6.8 %finish.1 = (bf16[512,1024]{1,0:T(8,128)(2,1)}, bf16[512,1024]{1,0:T(8,128)(2,1)}, bf16[512,1024]{1,0:T(8,128)(2,1)}, f32[1024,2048]{1,0:T(8,128)}) custom-call(bf16[512,1024]{1,0:T(8,128)(2,1)} %get-tuple-element.8.gq_in, bf16[512,1024]{1,0:T(8,128)(2,1)} %get-tuple-element.9.gk_in, bf16[512,1024]{1,0:T(8,128)(2,1)} %get-tuple-element.10.gv_in, ...), custom_call_target="tpu_custom_call" | custom-call | tf_op jit(solution)/shard_map/finish/pallas_call | solution.py:725

commit v4 on v3

--- a/solution.py
+++ b/solution.py
@@ -23,7 +23,7 @@
 ORDERS = (
     (1, 0, 2), (0, 1, 2), (2, 0, 1), (1, 0, 2), (0, 1, 2), (2, 1, 0), (1, 2, 0), (0, 2, 1),
 )
-NSEM = 232
+NSEM = 280
 BF = jnp.bfloat16
 F32 = jnp.float32
 SCALE = 1.0 / math.sqrt(WIDTH)
@@ -154,30 +154,43 @@
     for load in loads:
         load.start()
 
-    def near_at(c):
-        return lambda: nf.at[:, pl.ds(32 * c, 32), :]
-
-    def far_at(d):
-        return lambda: nf.at[:, pl.ds(FAR + 32 * d, 32), :]
-
-    def sib_at(first, rows):
-        return lambda: nf.at[:, pl.ds(HALF + first, rows), :]
+    def heads(u):
+        return range(UNITS[u][0], UNITS[u][0] + UNITS[u][1])
+
+    def span(u):
+        return pl.ds(*UNITS[u])
+
+    def columns(u):
+        return pl.ds(UNITS[u][0] * WIDTH, UNITS[u][1] * WIDTH)
+
+    def near_at(c, u):
+        return lambda: nf.at[:, pl.ds(32 * c, 32), columns(u)]
+
+    def far_at(d, u):
+        return lambda: nf.at[:, pl.ds(FAR + 32 * d, 32), columns(u)]
+
+    def sib_at(first, u):
+        return lambda: nf.at[:, pl.ds(HALF + first, 32), columns(u)]
 
     own_gather = [
         sems.copy(lambda: zsend, lambda m=m: zrecv.at[m], lambda m=m: me.cross(m))
         for m in range(1, 16)
     ]
     y_gather = [
-        sems.copy(far_at(0), far_at(d), lambda d=d: me.along(1, d)) for d in range(1, 4)
+        [sems.copy(far_at(0, u), far_at(d, u), lambda d=d: me.along(1, d)) for d in range(1, 4)]
+        for u in range(3)
     ]
     near_gather = [
-        sems.copy(near_at(0), near_at(c), lambda c=c: me.chip(c)) for c in range(1, CHIPS)
+        [sems.copy(near_at(0, u), near_at(c, u), lambda c=c: me.chip(c)) for c in range(1, CHIPS)]
+        for u in range(3)
     ]
     near_forward = [
-        sems.copy(near_at(c), sib_at(32 * c, 32), me.sibling) for c in range(CHIPS)
+        [sems.copy(near_at(c, u), sib_at(32 * c, u), me.sibling) for c in range(CHIPS)]
+        for u in range(3)
     ]
     far_forward = [
-        sems.copy(far_at(d), sib_at(FAR + 32 * d, 32), me.sibling) for d in range(4)
+        [sems.copy(far_at(d, u), sib_at(FAR + 32 * d, u), me.sibling) for d in range(4)]
+        for u in range(3)
     ]
 
     rows = lax.broadcasted_iota(jnp.int32, (32, ROWS), 0)
@@ -200,8 +213,9 @@
 
     pl.semaphore_wait(barrier, len(partners))
     start(own_gather)
-    start(near_gather)
-    near_forward[0].start()
+    for u in range(3):
+        start(near_gather[u])
+        near_forward[u][0].start()
 
     def project(i, carry):
         r = pl.ds(pl.multiple_of(i * 256, 256), 256)
@@ -221,29 +235,28 @@
                     4 * part + 2 * i : 4 * part + 2 * i + 2
                 ]
     nf[:, FAR : FAR + 32, :] = xblk[...].astype(BF)
-    start(y_gather)
-    far_forward[0].start()
+    for u in range(3):
+        start(y_gather[u])
+        far_forward[u][0].start()
     loads[4].wait()
-    for c in range(1, CHIPS):
-        near_gather[c - 1].wait()
-        near_forward[c].start()
-    for d in range(1, 4):
-        y_gather[d - 1].wait()
-        far_forward[d].start()
-    wait(near_forward)
-    wait(far_forward)
+
+    def gather_near(u):
+        for c in range(1, CHIPS):
+            near_gather[u][c - 1].wait()
+            near_forward[u][c].start()
+
+    def gather_far(u):
+        for d in range(1, 4):
+            y_gather[u][d - 1].wait()
+            far_forward[u][d].start()
+        wait(near_forward[u])
+        wait(far_forward[u])
+
+    gather_near(0)
+    gather_far(0)
 
     mine = pl.multiple_of(core * 64, 64)
     other = pl.multiple_of((1 - core) * 64, 64)
-
-    def heads(u):
-        return range(UNITS[u][0], UNITS[u][0] + UNITS[u][1])
-
-    def span(u):
-        return pl.ds(*UNITS[u])
-
-    def columns(u):
-        return pl.ds(UNITS[u][0] * WIDTH, UNITS[u][1] * WIDTH)
 
     def offsets(unit, first=0):
         return [
@@ -585,9 +598,11 @@
     scheduled(
         forward,
         {
-            2: [(weigh, 0)],
+            1: [(gather_near, 1)],
+            2: [(gather_far, 1), (weigh, 0)],
             3: [(weight_core, 0)],
-            5: [(weigh, 1)],
+            4: [(gather_near, 2)],
+            5: [(gather_far, 2), (weigh, 1)],
             6: [(weight_core, 1)],
             7: [(weight_a, 0), (weigh, 2)],
         },
@@ -598,39 +613,38 @@
             0: [(weight_core, 2)],
             1: [(weight_a, 1)],
             2: [(near_send, 0), (weight_b, 0)],
-            3: [(near_core, 0)],
-            4: [(weight_a, 2), (weight_b, 1)],
-            5: [(near_send, 1), (weight_c, 0)],
+            3: [(near_core, 0), (weight_a, 2)],
+            4: [(weight_b, 1)],
+            5: [(near_send, 1), (weight_c, 0), (weight_b, 2)],
             6: [(near_core, 1), (weight_c, 1)],
-            7: [(near_send, 2), (weight_b, 2), (weight_gather, 0, 2), (near_z, 0)],
+            7: [(near_send, 2), (weight_c, 2), (weight_gather, 0, 2), (near_z, 0)],
         },
     )
     store_q = pltpu.make_async_copy(q_ref, gq_hbm, store_sem.at[3])
     store_q.start()
     near_core(2)
     weight_gather(1, 2)
+    weight_gather(0, 1)
+    weight_gather(2, 2)
     near_y(0)
-    weight_c(2)
-    weight_gather(0, 1)
     near_z(1)
     near_y(1)
     weight_gather(1, 1)
     near_y(2)
-    weight_gather(2, 2)
+    weight_gather(2, 1)
     near_z(2)
     weight_gather(0, 0)
-    weight_gather(1, 0)
     near_x(0)
     near_x(1)
-    weight_gather(2, 1)
-    weight_last(0)
-    weight_last(1)
+    weight_gather(1, 0)
     near_x(2)
     finish_rows()
     store_k = pltpu.make_async_copy(k_ref, gk_hbm, store_sem.at[4])
     store_v = pltpu.make_async_copy(v_ref, gv_hbm, store_sem.at[5])
     store_k.start()
     store_v.start()
+    weight_last(0)
+    weight_last(1)
     weight_gather(2, 0)
     weight_last(2)
     for copy in w_out + [store_q, store_k, store_v]:

time: 98.2 us -> 92.8 us (0.945)
  Pallas kernels: 96.2 us -> 90.8 us
    pallas_call x1, Pallas kernels: 89.3 us -> 84 us  [body(): pl.pallas_call(kernel, out_shape=(token_shape,) * 3 + (jax.ShapeDtypeStru...]
where the time goes in v4:
time: 92.8 us; the launch traced here: 91.4 us
  Pallas kernels  90.8 us (98%)
    pallas_call x1, Pallas kernels, body(): pl.pallas_call(kernel, out_shape=(token_shape,) * 3 + (jax.ShapeDtypeStru...  84 us
    pallas_call x1, Pallas kernels, body(): pl.pallas_call(functools.partial(finish, 1.0 / math.sqrt(tokens)), out_sh...  6.81 us

profile of v4, /device:TPU:0, one launch (start us, length us, event | category | flops | bytes accessed | tf_op | source)
XLA Modules:
  0.0 91.4 jit_solution(10307320128176951185)
XLA Ops:
  0.6 84.0 %fused.1 = (bf16[512,1024]{1,0:T(8,128)(2,1)}, bf16[512,1024]{1,0:T(8,128)(2,1)}, bf16[512,1024]{1,0:T(8,128)(2,1)}, bf16[8,128,2048]{2,1,0:T(8,128)(2,1)}) custom-call(bf16[512,1024]{1,0:T(8,128)(2,1)} %q_hbm.1, bf16[512,1024]{1,0:T(8,128)(2,1)} %k_hbm.1, bf16[512,1024]{1,0:T(8,128)(2,1)} %v_hbm.1, bf16[512,2048]{1,0:T(8,128)(2,1)} %go_hbm.1, ...), custom_call_target="tpu_custom_call" | custom-call | tf_op jit(solution)/shard_map/fused/pallas_call | solution.py:727
  84.6 6.8 %finish.1 = (bf16[512,1024]{1,0:T(8,128)(2,1)}, bf16[512,1024]{1,0:T(8,128)(2,1)}, bf16[512,1024]{1,0:T(8,128)(2,1)}, f32[1024,2048]{1,0:T(8,128)}) custom-call(bf16[512,1024]{1,0:T(8,128)(2,1)} %get-tuple-element.8.gq_in, bf16[512,1024]{1,0:T(8,128)(2,1)} %get-tuple-element.9.gk_in, bf16[512,1024]{1,0:T(8,128)(2,1)} %get-tuple-element.10.gv_in, ...), custom_call_target="tpu_custom_call" | custom-call | tf_op jit(solution)/shard_map/finish/pallas_call | solution.py:739

commit v5 on v4

--- a/solution.py
+++ b/solution.py
@@ -611,29 +611,29 @@
         backward,
         {
             0: [(weight_core, 2)],
-            1: [(weight_a, 1)],
-            2: [(near_send, 0), (weight_b, 0)],
-            3: [(near_core, 0), (weight_a, 2)],
-            4: [(weight_b, 1)],
-            5: [(near_send, 1), (weight_c, 0), (weight_b, 2)],
-            6: [(near_core, 1), (weight_c, 1)],
-            7: [(near_send, 2), (weight_c, 2), (weight_gather, 0, 2), (near_z, 0)],
+            1: [(weight_a, 1), (weight_b, 0)],
+            2: [(near_send, 0)],
+            3: [(weight_c, 0), (weight_a, 2), (weight_b, 1), (near_core, 0)],
+            5: [(near_send, 1), (weight_gather, 0, 2), (weight_c, 1), (weight_b, 2)],
+            6: [(near_core, 1)],
+            7: [
+                (near_send, 2), (weight_gather, 0, 1), (weight_gather, 1, 2), (weight_c, 2),
+                (near_z, 0),
+            ],
         },
     )
     store_q = pltpu.make_async_copy(q_ref, gq_hbm, store_sem.at[3])
     store_q.start()
     near_core(2)
-    weight_gather(1, 2)
-    weight_gather(0, 1)
     weight_gather(2, 2)
+    weight_gather(1, 1)
     near_y(0)
     near_z(1)
     near_y(1)
-    weight_gather(1, 1)
+    weight_gather(2, 1)
     near_y(2)
-    weight_gather(2, 1)
+    weight_gather(0, 0)
     near_z(2)
-    weight_gather(0, 0)
     near_x(0)
     near_x(1)
     weight_gather(1, 0)

time: 92.8 us -> 92.5 us (level)
  no operation moved by 1% of the time
where the time goes in v5:
time: 92.5 us; the launch traced here: 91.2 us
  Pallas kernels  90.6 us (98%)
    pallas_call x1, Pallas kernels, body(): pl.pallas_call(kernel, out_shape=(token_shape,) * 3 + (jax.ShapeDtypeStru...  83.8 us
    pallas_call x1, Pallas kernels, body(): pl.pallas_call(functools.partial(finish, 1.0 / math.sqrt(tokens)), out_sh...  6.81 us

profile of v5, /device:TPU:0, one launch (start us, length us, event | category | flops | bytes accessed | tf_op | source)
XLA Modules:
  0.0 91.2 jit_solution(11199624554415044789)
XLA Ops:
  0.6 83.8 %fused.1 = (bf16[512,1024]{1,0:T(8,128)(2,1)}, bf16[512,1024]{1,0:T(8,128)(2,1)}, bf16[512,1024]{1,0:T(8,128)(2,1)}, bf16[8,128,2048]{2,1,0:T(8,128)(2,1)}) custom-call(bf16[512,1024]{1,0:T(8,128)(2,1)} %q_hbm.1, bf16[512,1024]{1,0:T(8,128)(2,1)} %k_hbm.1, bf16[512,1024]{1,0:T(8,128)(2,1)} %v_hbm.1, bf16[512,2048]{1,0:T(8,128)(2,1)} %go_hbm.1, ...), custom_call_target="tpu_custom_call" | custom-call | tf_op jit(solution)/shard_map/fused/pallas_call | solution.py:727
  84.4 6.8 %finish.1 = (bf16[512,1024]{1,0:T(8,128)(2,1)}, bf16[512,1024]{1,0:T(8,128)(2,1)}, bf16[512,1024]{1,0:T(8,128)(2,1)}, f32[1024,2048]{1,0:T(8,128)}) custom-call(bf16[512,1024]{1,0:T(8,128)(2,1)} %get-tuple-element.8.gq_in, bf16[512,1024]{1,0:T(8,128)(2,1)} %get-tuple-element.9.gk_in, bf16[512,1024]{1,0:T(8,128)(2,1)} %get-tuple-element.10.gv_in, ...), custom_call_target="tpu_custom_call" | custom-call | tf_op jit(solution)/shard_map/finish/pallas_call | solution.py:739

commit v6 on v5

--- a/solution.py
+++ b/solution.py
@@ -181,7 +181,8 @@
         for u in range(3)
     ]
     near_gather = [
-        [sems.copy(near_at(0, u), near_at(c, u), lambda c=c: me.chip(c)) for c in range(1, CHIPS)]
+        [sems.copy(near_at(0, u), near_at(c, u), lambda c=c: me.chip(c)) for c in range(1, 5)]
+        + [sems.copy(near_at(4, u), near_at(4 + d, u), lambda d=d: me.along(2, d)) for d in range(1, 4)]
         for u in range(3)
     ]
     near_forward = [
@@ -214,7 +215,7 @@
     pl.semaphore_wait(barrier, len(partners))
     start(own_gather)
     for u in range(3):
-        start(near_gather[u])
+        start(near_gather[u][:4])
         near_forward[u][0].start()
 
     def project(i, carry):
@@ -225,6 +226,13 @@
     loads[2].wait()
     loads[3].wait()
     lax.fori_loop(0, 4, project, 0)
+
+    def relay(u):
+        near_gather[u][3].wait()
+        start(near_gather[u][4:])
+        near_forward[u][4].start()
+
+    relay(0)
 
     wait(own_gather)
     for m in range(16):
@@ -239,9 +247,11 @@
         start(y_gather[u])
         far_forward[u][0].start()
     loads[4].wait()
+    relay(1)
+    relay(2)
 
     def gather_near(u):
-        for c in range(1, CHIPS):
+        for c in (1, 2, 3, 5, 6, 7):
             near_gather[u][c - 1].wait()
             near_forward[u][c].start()
 

time: 92.5 us -> 94.2 us (1.018)
  Pallas kernels: 90.6 us -> 92.2 us
    pallas_call x1, Pallas kernels: 83.8 us -> 85.4 us  [body(): pl.pallas_call(kernel, out_shape=(token_shape,) * 3 + (jax.ShapeDtypeStru...]
where the time goes in v6:
time: 94.2 us; the launch traced here: 92.8 us
  Pallas kernels  92.2 us (98%)
    pallas_call x1, Pallas kernels, body(): pl.pallas_call(kernel, out_shape=(token_shape,) * 3 + (jax.ShapeDtypeStru...  85.4 us
    pallas_call x1, Pallas kernels, body(): pl.pallas_call(functools.partial(finish, 1.0 / math.sqrt(tokens)), out_sh...  6.81 us

profile of v6, /device:TPU:0, one launch (start us, length us, event | category | flops | bytes accessed | tf_op | source)
XLA Modules:
  0.0 92.8 jit_solution(11915094741885368528)
XLA Ops:
  0.6 85.4 %fused.1 = (bf16[512,1024]{1,0:T(8,128)(2,1)}, bf16[512,1024]{1,0:T(8,128)(2,1)}, bf16[512,1024]{1,0:T(8,128)(2,1)}, bf16[8,128,2048]{2,1,0:T(8,128)(2,1)}) custom-call(bf16[512,1024]{1,0:T(8,128)(2,1)} %q_hbm.1, bf16[512,1024]{1,0:T(8,128)(2,1)} %k_hbm.1, bf16[512,1024]{1,0:T(8,128)(2,1)} %v_hbm.1, bf16[512,2048]{1,0:T(8,128)(2,1)} %go_hbm.1, ...), custom_call_target="tpu_custom_call" | custom-call | tf_op jit(solution)/shard_map/fused/pallas_call | solution.py:737
  86.0 6.8 %finish.1 = (bf16[512,1024]{1,0:T(8,128)(2,1)}, bf16[512,1024]{1,0:T(8,128)(2,1)}, bf16[512,1024]{1,0:T(8,128)(2,1)}, f32[1024,2048]{1,0:T(8,128)}) custom-call(bf16[512,1024]{1,0:T(8,128)(2,1)} %get-tuple-element.8.gq_in, bf16[512,1024]{1,0:T(8,128)(2,1)} %get-tuple-element.9.gk_in, bf16[512,1024]{1,0:T(8,128)(2,1)} %get-tuple-element.10.gv_in, ...), custom_call_target="tpu_custom_call" | custom-call | tf_op jit(solution)/shard_map/finish/pallas_call | solution.py:749
